TPU v7x, 128 devices: a whole 4x4x4 slice. The times are simulated.
128 devices in a mesh: ctx: 8 (over z, y_lo), head: 4 (over x), dp: 4 (over y_hi, core).
Axes of the slice: x: 4, y: 4 (y_hi: 2, y_lo: 2; y = y_hi * 2 + y_lo), z: 4, core: 2. Of those that a mesh axis runs over, the one named last changes fastest.
Arguments:
- patch_rows: bfloat16 [24576, 3072], P(('dp', 'ctx'), 'head'), parts along dimension 0, may hold values from -40 to 40
- query_weight: bfloat16 [3072, 3072], P(None, 'head'), may hold values from -0.109375 to 0.109375
- key_weight: bfloat16 [3072, 3072], P(None, 'head'), may hold values from -0.109375 to 0.109375
- value_weight: bfloat16 [3072, 3072], P(None, 'head'), may hold values from -0.109375 to 0.109375
- output_weight: bfloat16 [3072, 3072], P('head'), may hold values from -0.109375 to 0.109375
- tile_slot: int32 [192], P('dp'), parts along dimension 0, may hold values from 0 to 47, as said below
- tile_mask: int32 [192, 48], P('dp'), parts along dimension 0, may hold values from 0 to 1, as said below
Outputs:
- layer_output: bfloat16 [24576, 3072], P(('dp', 'ctx'), 'head'), parts along dimension 0
There are 4 independent parts, one for each index of `dp`. A program takes and returns all parts, laid end to end along the dimension named above; an argument that names none is the same for every part. Nothing has to cross between parts.
Inputs may be any that keep to these rules, and one draw needn't show every extreme that they name: A permutation: loader tile t (rows t*128 to (t+1)*128 - 1 of patch_rows, on loader shard t // 6) becomes context tile tile_slot[t]; context shard c holds context tiles c*6 to (c+1)*6 - 1. The tiles of one loader shard are spread as evenly over the context shards as they can be, so that every loader shard sends exactly 1 tiles to some context shard and none sends more. `tile_mask`: 1 only where both tiles lie in one clip, a run of consecutive context tiles; every tile is live for itself; one clip covers half of the tiles or more.
All inputs are finite; a program needn't handle non-finite values.
Results may differ from a plain program's by a relative error of at most 0.015.
The roundings to bfloat16 on the way count: a program that leaves them out, or rounds other values in their place, can miss the bound.
Values may be sent and summed in bfloat16 or wider, within the bound.
A program may use at most 128 MiB of HBM per device.

v0:
```python
import math

import jax
import jax.numpy as jnp
from jax import lax
from jax.sharding import PartitionSpec as P

HDIM = 128
TILE = 128


MASKED = -1e30


def route_tables(tile_slot, shard_index, tile_count, groups, capacity):
    slot_grid = tile_slot.reshape(groups, tile_count)
    target = slot_grid // tile_count
    earlier = jnp.tril(jnp.ones((tile_count, tile_count), jnp.int32), -1)
    same_target = (target[:, :, None] == target[:, None, :]).astype(jnp.int32)
    bucket_rank = jnp.sum(same_target * earlier[None, :, :], axis=2)
    bucket_ids = jnp.arange(groups * capacity, dtype=jnp.int32)
    own_bucket = lax.dynamic_index_in_dim(
        target * capacity + bucket_rank, shard_index, 0, keepdims=False
    )
    send_table = (bucket_ids[:, None] == own_bucket[None, :]).astype(jnp.bfloat16)
    source = jnp.arange(groups, dtype=jnp.int32)[:, None]
    arrival = (source * capacity + bucket_rank).reshape(-1)
    landing = (slot_grid - shard_index * tile_count).reshape(-1)
    arrives_here = (target == shard_index).reshape(-1)
    places = jnp.arange(tile_count, dtype=jnp.int32)
    matches = (
        (landing[None, None, :] == places[:, None, None])
        & (arrival[None, None, :] == bucket_ids[None, :, None])
        & arrives_here[None, None, :]
    )
    recv_table = jnp.any(matches, axis=2).astype(jnp.bfloat16)
    return (send_table, recv_table)


def place_tiles(route_table, tile_boxes):
    return jnp.einsum(
        "ab,btf->atf", route_table, tile_boxes, preferred_element_type=jnp.float32
    ).astype(jnp.bfloat16)


def to_tiles(route_table, row_block):
    return place_tiles(route_table, row_block.reshape(-1, TILE, row_block.shape[1]))


def from_tiles(route_table, tile_boxes):
    return place_tiles(route_table, tile_boxes).reshape(-1, tile_boxes.shape[2])


def project(features, weight):
    return jnp.dot(features, weight, preferred_element_type=jnp.float32).astype(jnp.bfloat16)


def body(patch_rows, query_weight, key_weight, value_weight, output_weight, tile_slot, tile_mask):
    groups = lax.axis_size("ctx")
    shard_index = lax.axis_index("ctx")
    tok_dev = patch_rows.shape[0]
    tile_count = tok_dev // TILE
    capacity = (tile_count + groups - 1) // groups
    send_table, recv_table = route_tables(tile_slot, shard_index, tile_count, groups, capacity)
    features = lax.all_gather(patch_rows, "head", axis=1, tiled=True)
    moved_query, moved_key, moved_value = (
        lax.all_to_all(
            to_tiles(send_table, project(features, query_weight)),
            "ctx",
            split_axis=0,
            concat_axis=0,
            tiled=True,
        ),
        lax.all_to_all(
            to_tiles(send_table, project(features, key_weight)),
            "ctx",
            split_axis=0,
            concat_axis=0,
            tiled=True,
        ),
        lax.all_to_all(
            to_tiles(send_table, project(features, value_weight)),
            "ctx",
            split_axis=0,
            concat_axis=0,
            tiled=True,
        ),
    )
    query_rows = from_tiles(recv_table, moved_query)
    key_rows = from_tiles(recv_table, moved_key)
    value_rows = from_tiles(recv_table, moved_value)
    heads_dev = query_rows.shape[1] // HDIM
    score_scale = 1.0 / math.sqrt(HDIM)

    def by_heads(row_block):
        return row_block.reshape(tok_dev, heads_dev, HDIM).transpose(1, 0, 2)

    queries = by_heads(query_rows)
    key_heads = by_heads(key_rows)
    value_heads = by_heads(value_rows)
    tile_total = tile_mask.shape[1]
    mask_rows = lax.dynamic_slice_in_dim(tile_mask, shard_index * tile_count, tile_count, 0).astype(
        jnp.float32
    )
    start_state = (
        jnp.full((heads_dev, tok_dev), MASKED, jnp.float32),
        jnp.zeros((heads_dev, tok_dev), jnp.float32),
        jnp.zeros((heads_dev, tok_dev, HDIM), jnp.float32),
    )
    key_piece = lax.all_gather(key_heads, "ctx", axis=1, tiled=True)
    value_piece = lax.all_gather(value_heads, "ctx", axis=1, tiled=True)
    key_count = key_piece.shape[1]
    key_tile = jnp.arange(key_count, dtype=jnp.int32) // TILE
    picker = (jnp.arange(tile_total, dtype=jnp.int32)[:, None] == key_tile[None, :]).astype(
        jnp.float32
    )
    live_tiles = jnp.dot(mask_rows, picker) > 0.5
    live_rows = jnp.broadcast_to(live_tiles[:, None, :], (tile_count, TILE, key_count)).reshape(
        tok_dev, key_count
    )

    def one_head(inputs):
        old_peak, weight_sum, summed, query_head, key_head, value_head = inputs
        scores = (
            jnp.einsum("qd,kd->qk", query_head, key_head, preferred_element_type=jnp.float32)
            * score_scale
        )
        new_peak = jnp.maximum(old_peak, jnp.max(jnp.where(live_rows, scores, MASKED), axis=1))
        weights = jnp.where(live_rows, jnp.exp(scores - new_peak[:, None]), 0.0)
        shrink = jnp.exp(old_peak - new_peak)
        weight_sum = weight_sum * shrink + jnp.sum(weights, axis=1)
        summed = summed * shrink[:, None] + jnp.dot(
            weights.astype(jnp.bfloat16), value_head, preferred_element_type=jnp.float32
        )
        return (new_peak, weight_sum, summed)

    result = lax.map(
        one_head, (start_state[0], start_state[1], start_state[2], queries, key_piece, value_piece)
    )
    final_peak, weight_sum, summed = result
    attended = (
        (summed / weight_sum[:, :, None])
        .transpose(1, 0, 2)
        .reshape(tok_dev, heads_dev * HDIM)
        .astype(jnp.bfloat16)
    )
    partial_out = jnp.dot(attended, output_weight, preferred_element_type=jnp.float32)
    mixed_rows = lax.psum_scatter(
        partial_out.astype(jnp.bfloat16), "head", scatter_dimension=1, tiled=True
    )
    sent_back = lax.all_to_all(
        to_tiles(recv_table.T, mixed_rows), "ctx", split_axis=0, concat_axis=0, tiled=True
    )
    return from_tiles(send_table.T, sent_back)


def solution(mesh):
    in_specs = (
        P(("dp", "ctx"), "head"),
        P(None, "head"),
        P(None, "head"),
        P(None, "head"),
        P("head", None),
        P("dp"),
        P("dp", None),
    )
    out_specs = P(("dp", "ctx"), "head")
    return jax.shard_map(body, mesh=mesh, in_specs=in_specs, out_specs=out_specs, check_vma=False)
```

profile of v0, /device:TPU:1, one launch (start us, length us, event | category | flops | bytes accessed | tf_op | source)
XLA Modules:
  0.0 702.6 jit_solution(10393103524887853727)
XLA Ops:
  8.9 55.9 %all-gather.4.cloned.1.call-done = bf16[768,3072]{1,0:T(8,128)(2,1)} async-done(((bf16[768,768]{1,0:T(8,128)(2,1)}), bf16[768,3072]{1,0:T(8,128)(2,1)}) %all-gather.4.cloned.1.call-update) | async-done | bytes 4718608 | tf_op jit(solution)/shard_map/all_gather | solution.py:65
  64.8 7.6 %convolution_convert_fusion.10 = bf16[768,768]{1,0:T(8,128)(2,1)S(1)} fusion(bf16[768,3072]{1,0:T(8,128)(2,1)} %all-gather.4.cloned.1.call-done, bf16[3072,768]{1,0:T(8,128)(2,1)} %param.11), kind=kOutput, calls=%fused_computation.42 | convolution fusion | flops 3624468480 | bytes 10616832 | tf_op jit(solution)/shard_map/dot_general | solution.py:55
  72.4 1.0 convolution_convert_fusion.6
  73.4 1.4 copy.83
  74.9 5.2 all-to-all-start.1
  80.5 20.0 %all-to-all-done.1 = bf16[8,128,768]{2,1,0:T(8,128)(2,1)S(1)} async-done(((bf16[8,128,768]{2,1,0:T(8,128)(2,1)}), bf16[8,128,768]{2,1,0:T(8,128)(2,1)S(1)}, u32[]{:S(2)}, u32[]{:S(2)}) %all-to-all-start.1) | async-done | bytes 1572896 | tf_op jit(solution)/shard_map/all_to_all | solution.py:74
  101.7 1.4 reshape_reshape.10
  103.1 1.2 copy.86
  104.4 7.6 %convolution_convert_fusion.9 = bf16[768,768]{1,0:T(8,128)(2,1)S(1)} fusion(bf16[768,3072]{1,0:T(8,128)(2,1)} %all-gather.4.cloned.1.call-done, bf16[3072,768]{1,0:T(8,128)(2,1)} %param.12), kind=kOutput, calls=%fused_computation.41 | convolution fusion | flops 3624468480 | bytes 10616832 | tf_op jit(solution)/shard_map/dot_general | solution.py:55
  111.9 1.0 convolution_convert_fusion.4
  113.3 42.0 %all_to_all.20 = bf16[8,128,768]{2,1,0:T(8,128)(2,1)S(1)} all-to-all(bf16[8,128,768]{2,1,0:T(8,128)(2,1)S(1)} %copy.89), channel_id=1, replica_groups=mesh['ctx'=8,'head'=4,'dp'=4] {'ctx'}, dimensions={0} | all-to-all | bytes 3145728 | tf_op jit(solution)/shard_map/all_to_all | solution.py:81
  156.5 1.4 reshape_reshape.11
  157.8 1.2 copy.92
  159.1 7.6 %convolution_convert_fusion.11 = bf16[768,768]{1,0:T(8,128)(2,1)S(1)} fusion(bf16[768,3072]{1,0:T(8,128)(2,1)} %all-gather.4.cloned.1.call-done, bf16[3072,768]{1,0:T(8,128)(2,1)} %param.10), kind=kOutput, calls=%fused_computation.43 | convolution fusion | flops 3624468480 | bytes 10616832 | tf_op jit(solution)/shard_map/dot_general | solution.py:55
  166.6 1.0 convolution_convert_fusion.8
  167.7 1.5 copy.78
  169.1 3.6 all-to-all-start
  172.8 1.0 convolution_compare_fusion
  173.8 36.9 %all-to-all-done = bf16[8,128,768]{2,1,0:T(8,128)(2,1)S(1)} async-done(((bf16[8,128,768]{2,1,0:T(8,128)(2,1)}), bf16[8,128,768]{2,1,0:T(8,128)(2,1)S(1)}, u32[]{:S(2)}, u32[]{:S(2)}) %all-to-all-start) | async-done | bytes 1572896 | tf_op jit(solution)/shard_map/all_to_all | solution.py:67
  211.9 1.4 reshape_reshape.9
  213.5 112.2 %all-gather.6.cloned.1.call-done = bf16[6,6144,128]{2,1,0:T(8,128)(2,1)} async-done(((bf16[6,768,128]{2,1,0:T(8,128)(2,1)}), bf16[6,6144,128]{2,1,0:T(8,128)(2,1)}) %all-gather.6.cloned.1.call-update) | async-done | bytes 9437200 | tf_op jit(solution)/shard_map/all_gather | solution.py:110
  325.7 190.8 %all-gather.8.cloned.1.call-done = bf16[6,6144,128]{2,1,0:T(8,128)(2,1)} async-done(((bf16[6,768,128]{2,1,0:T(8,128)(2,1)}), bf16[6,6144,128]{2,1,0:T(8,128)(2,1)}) %all-gather.8.cloned.1.call-update) | async-done | bytes 9437200 | tf_op jit(solution)/shard_map/all_gather | solution.py:111
  516.4 87.2 %while.13 = (s32[]{:T(128)}, f32[6,768]{1,0:T(8,128)S(1)}, f32[6,768,128]{1,2,0:T(8,128)}, bf16[6,768,128]{2,1,0:T(8,128)(2,1)S(1)}, bf16[6,6144,128]{2,1,0:T(8,...) while((s32[]{:T(128)}, f32[6,768]{1,0:T(8,128)S(1)}, ...), condition=%wide.region_5.6_spmd.clone, body=%wide.region_2.5_spmd.clone.sunk | while | flops 2453768448 | bytes 62062688 | solution.py:137
  516.4 4.4 fusion.68
  520.9 4.9 fusion.69
  525.8 4.1 fusion.70
  531.0 4.5 fusion.68
  535.4 4.9 fusion.69
  540.4 4.1 fusion.70
  545.5 4.5 fusion.68
  550.0 4.9 fusion.69
  554.9 4.1 fusion.70
  560.1 4.5 fusion.68
  564.5 4.9 fusion.69
  569.5 4.1 fusion.70
  574.6 4.5 fusion.68
  579.1 4.9 fusion.69
  584.0 4.1 fusion.70
  589.1 4.5 fusion.68
  593.6 4.9 fusion.69
  598.5 4.1 fusion.70
  603.6 1.9 divide_convert_fusion
  605.5 7.9 %convolution_convert_fusion = bf16[768,3072]{1,0:T(8,128)(2,1)} fusion(bf16[768,768]{0,1:T(8,128)(2,1)S(1)} %bitcast.88, bf16[768,3072]{1,0:T(8,128)(2,1)} %param.13), kind=kOutput, calls=%fused_computation.23 | convolution fusion | flops 3626237952 | bytes 10616832 | tf_op jit(solution)/shard_map/dot_general | solution.py:147
  613.4 52.3 %reduce-scatter.2.cloned.1.call-done = bf16[768,768]{1,0:T(8,128)(2,1)} async-done(((bf16[768,3072]{1,0:T(8,128)(2,1)}), bf16[768,768]{1,0:T(8,128)(2,1)}) %reduce-scatter.2.cloned.1.call-update) | async-done | bytes 1179664 | tf_op jit(solution)/shard_map/reduce_scatter | solution.py:148
  665.7 2.2 convolution_convert_fusion.2
  668.2 25.6 %all_to_all.21 = bf16[8,128,768]{2,1,0:T(8,128)(2,1)S(1)} all-to-all(bf16[8,128,768]{2,1,0:T(8,128)(2,1)S(1)} %copy.97), channel_id=1, replica_groups=mesh['ctx'=8,'head'=4,'dp'=4] {'ctx'}, dimensions={0} | all-to-all | bytes 3145728 | tf_op jit(solution)/shard_map/all_to_all | solution.py:151
  693.8 1.0 convolution_convert_fusion.1
  694.8 1.2 copy.99
  (76 shorter events, 13.4 us)
Async XLA Ops:
  6.5 58.3 %all-gather.4.cloned.1.call-start = ((), (), s32[]{:S(2)}) async-start(), calls=%async_computation.5 | async-start | bytes 5898240 | tf_op jit(solution)/shard_map/all_gather | solution.py:65
  74.9 5.4 copy-start
  74.9 25.6 %all-to-all-start.1 = ((bf16[8,128,768]{2,1,0:T(8,128)(2,1)}), bf16[8,128,768]{2,1,0:T(8,128)(2,1)S(1)}, u32[]{:S(2)}, u32[]{:S(2)}) async-start(bf16[8,128,768]{2,1,0:T(8,128)(2,1)} %copy.83), calls=%async_computation.1 | async-start | bytes 3145728 | tf_op jit(solution)/shard_map/all_to_all | solution.py:74
  80.1 245.6 %all-gather.6.cloned.1.call-start = ((), (), s32[]{:S(2)}) async-start(), calls=%async_computation.6 | async-start | bytes 10616832 | tf_op jit(solution)/shard_map/all_gather | solution.py:110
  104.3 412.1 %all-gather.8.cloned.1.call-start = ((), (), s32[]{:S(2)}) async-start(), calls=%async_computation.7 | async-start | bytes 10616832 | tf_op jit(solution)/shard_map/all_gather | solution.py:111
  169.1 41.6 %all-to-all-start = ((bf16[8,128,768]{2,1,0:T(8,128)(2,1)}), bf16[8,128,768]{2,1,0:T(8,128)(2,1)S(1)}, u32[]{:S(2)}, u32[]{:S(2)}) async-start(bf16[8,128,768]{2,1,0:T(8,128)(2,1)} %copy.78), calls=%async_computation | async-start | bytes 3145728 | tf_op jit(solution)/shard_map/all_to_all | solution.py:67
  172.7 493.0 %reduce-scatter.2.cloned.1.call-start = ((), (), s32[]{:S(2)}) async-start(), calls=%async_computation.8 | async-start | bytes 5898240 | tf_op jit(solution)/shard_map/reduce_scatter | solution.py:148
Sparse Core Ops, SparseCore 0:
  9.0 55.7 all-gather.3
  104.4 221.2 all-gather.5
  327.3 189.0 all-gather.7
  613.5 52.1 reduce-scatter.1
where the time goes:
time: 704 us; the launch traced here: 703 us
  waiting for transfers between devices  469 us (67%)
  matrix products  92.2 us (13%)
  blocking collectives  67.5 us (10%)
  other arithmetic  32.6 us (5%)
  local copies, waits for them, and re-layouts  18.8 us (3%)
  between operations  13.4 us (2%)
  starting transfers between devices  8.9 us (1%)
    all_gather x1, waiting for transfers between devices, body(): value_piece = lax.all_gather(value_heads, 'ctx', axis=1, tiled=True)  191 us
    all_gather x1, waiting for transfers between devices, body(): key_piece = lax.all_gather(key_heads, 'ctx', axis=1, tiled=True)  112 us
    all_gather x1, waiting for transfers between devices, body(): features = lax.all_gather(patch_rows, 'head', axis=1, tiled=True)  55.9 us
    reduce_scatter x1, waiting for transfers between devices, body(): lax.psum_scatter(partial_out.astype(jnp.bfloat16), 'head', scatter_dimens...  52.3 us
    all_to_all x1, blocking collectives, body(): lax.all_to_all(to_tiles(send_table, project(features, value_weight)), 'ct...  42 us
    all_to_all x1, waiting for transfers between devices, body(): lax.all_to_all(to_tiles(send_table, project(features, query_weight)), 'ct...  36.9 us
    convert_element_type x6, other arithmetic, one_head(): weights.astype(jnp.bfloat16)  29.4 us
    dot_general x6, matrix products, one_head(): jnp.einsum('qd,kd->qk', query_head, key_head, preferred_element_type=jnp....  26.7 us
  transfers between devices with their start and end apart: 6, of which 6 were waited for; matrix products, arithmetic and copies ran while one was open for 4% of the time, Pallas kernels for 0%

commit v1 on v0

v1 whole, which is shorter than its diff:
```python
import math

import jax
import jax.numpy as jnp
from jax import lax
from jax.experimental import pallas as pl
from jax.experimental.pallas import tpu as pltpu
from jax.sharding import PartitionSpec as P

HDIM = 128
TILE = 128
GROUP = 4
LOG2E = 1.4426950408889634


def attend_kernel(
    key_list, value_list, counts, qkv_ref, out_ref, keys_t, values, scores
):
    tiles = qkv_ref.shape[0] // TILE
    pad = key_list.shape[0] // tiles
    factor = LOG2E / math.sqrt(HDIM)

    @pl.when(counts[tiles] == 1)
    def _():
        def prepare(t, carry):
            rows = pl.ds(pl.multiple_of(t * TILE, TILE), TILE)
            keys_t[:, rows] = qkv_ref[rows, HDIM : 2 * HDIM].T
            values[rows, :HDIM] = qkv_ref[rows, 2 * HDIM :]
            values[rows, HDIM:] = jnp.ones((TILE, HDIM), jnp.bfloat16)
            return carry

        lax.fori_loop(0, tiles, prepare, 0)
        values[pl.ds(tiles * TILE, TILE), :] = jnp.zeros((TILE, 2 * HDIM), jnp.bfloat16)

        def query_tile(t, carry):
            rows = pl.ds(pl.multiple_of(t * TILE, TILE), TILE)
            query = qkv_ref[rows, :HDIM]
            steps = (counts[t] + GROUP - 1) // GROUP

            def score_step(g, peak):
                base = t * pad + g * GROUP
                block = jnp.concatenate(
                    [
                        keys_t[:, pl.ds(pl.multiple_of(key_list[base + i] * TILE, TILE), TILE)]
                        for i in range(GROUP)
                    ],
                    axis=1,
                )
                found = jnp.dot(query, block, preferred_element_type=jnp.float32)
                scores[g] = found
                for i in range(GROUP):
                    peak = jnp.maximum(peak, found[:, i * TILE : (i + 1) * TILE])
                return peak

            peak = lax.fori_loop(
                0, steps, score_step, jnp.full((TILE, TILE), -jnp.inf, jnp.float32)
            )
            row_peak = jnp.max(peak, axis=1, keepdims=True) * factor

            def value_step(g, total):
                base = t * pad + g * GROUP
                weight = jnp.exp2(scores[g] * factor - row_peak).astype(jnp.bfloat16)
                block = jnp.concatenate(
                    [
                        values[pl.ds(pl.multiple_of(value_list[base + i] * TILE, TILE), TILE), :]
                        for i in range(GROUP)
                    ],
                    axis=0,
                )
                return total + jnp.dot(weight, block, preferred_element_type=jnp.float32)

            total = lax.fori_loop(
                0, steps, value_step, jnp.zeros((TILE, 2 * HDIM), jnp.float32)
            )
            out_ref[rows, :] = (total[:, :HDIM] / total[:, HDIM:]).astype(jnp.bfloat16)
            return carry

        lax.fori_loop(0, tiles, query_tile, 0)


def attend(key_list, value_list, counts, qkv):
    rows = qkv.shape[0]
    return pl.pallas_call(
        attend_kernel,
        out_shape=jax.ShapeDtypeStruct((rows, HDIM), jnp.bfloat16),
        grid_spec=pltpu.PrefetchScalarGridSpec(
            num_scalar_prefetch=3,
            grid=(1,),
            in_specs=[pl.BlockSpec((rows, 3 * HDIM), lambda i, *_: (0, 0))],
            out_specs=pl.BlockSpec((rows, HDIM), lambda i, *_: (0, 0)),
            scratch_shapes=[
                pltpu.VMEM((HDIM, rows), jnp.bfloat16),
                pltpu.VMEM((rows + TILE, 2 * HDIM), jnp.bfloat16),
                pltpu.VMEM((rows // (TILE * GROUP), TILE, GROUP * TILE), jnp.float32),
            ],
        ),
        compiler_params=pltpu.CompilerParams(vmem_limit_bytes=40 * 1024 * 1024),
        cost_estimate=pl.CostEstimate(
            flops=4 * rows * rows * HDIM, bytes_accessed=8 * rows * HDIM, transcendentals=rows * rows
        ),
        name="attend",
    )(key_list, value_list, counts, qkv)


def live_lists(tile_slot, tile_mask, active):
    tiles = tile_slot.shape[0]
    places = jnp.arange(tiles, dtype=jnp.int32)
    pick = (tile_slot[:, None] == places[None, :]).astype(jnp.float32)
    mask = (tile_mask == 1).astype(jnp.float32)
    live = jnp.dot(jnp.dot(pick, mask), pick.T)
    upper = (places[:, None] <= places[None, :]).astype(jnp.float32)
    rank = jnp.dot(live, upper).astype(jnp.int32) - 1
    counts = rank[:, -1] + 1
    hit = (rank[:, :, None] == places[None, None, :]) & (live[:, :, None] > 0.5)
    listed = jnp.sum(jnp.where(hit, places[None, :, None], 0), axis=1)
    used = places[None, :] < counts[:, None]
    key_list = jnp.where(used, listed, listed[:, :1]).reshape(-1)
    value_list = jnp.where(used, listed, tiles).reshape(-1)
    counts = jnp.concatenate([counts, active.astype(jnp.int32)[None]])
    return key_list, value_list, counts


def project(features, weight):
    return jnp.dot(features, weight, preferred_element_type=jnp.float32).astype(jnp.bfloat16)


def body(patch_rows, query_weight, key_weight, value_weight, output_weight, tile_slot, tile_mask):
    groups = lax.axis_size("ctx")
    shard = lax.axis_index("ctx")
    tokens = patch_rows.shape[0]
    heads = query_weight.shape[1] // HDIM
    slots = [0, 1, 2, 4, 5, 6]
    active = lax.rem(shard, 4) != 3
    key_list, value_list, counts = live_lists(tile_slot, tile_mask, active)
    features = lax.all_gather(patch_rows, "head", axis=1, tiled=True)
    query = project(features, query_weight)
    key = project(features, key_weight)
    value = project(features, value_weight)
    packs = []
    empty = jnp.zeros((tokens, 3 * HDIM), jnp.bfloat16)
    for s in range(groups):
        if s in slots:
            h = slots.index(s)
            cols = slice(h * HDIM, (h + 1) * HDIM)
            packs.append(jnp.concatenate([query[:, cols], key[:, cols], value[:, cols]], axis=1))
        else:
            packs.append(empty)
    sent = lax.all_to_all(jnp.stack(packs), "ctx", split_axis=0, concat_axis=0, tiled=True)
    attended = attend(key_list, value_list, counts, sent.reshape(groups * tokens, 3 * HDIM))
    back = lax.all_to_all(
        attended.reshape(groups, tokens, HDIM), "ctx", split_axis=0, concat_axis=0, tiled=True
    )
    attended = jnp.concatenate([back[s] for s in slots], axis=1)
    partial_out = jnp.dot(attended, output_weight, preferred_element_type=jnp.float32)
    return lax.psum_scatter(
        partial_out.astype(jnp.bfloat16), "head", scatter_dimension=1, tiled=True
    )


def solution(mesh):
    in_specs = (
        P(("dp", "ctx"), "head"),
        P(None, "head"),
        P(None, "head"),
        P(None, "head"),
        P("head", None),
        P("dp"),
        P("dp", None),
    )
    out_specs = P(("dp", "ctx"), "head")
    return jax.shard_map(body, mesh=mesh, in_specs=in_specs, out_specs=out_specs, check_vma=False)
```

time: 704 us -> 416 us (0.59)
  waiting for transfers between devices: 469 us -> 260 us
  Pallas kernels: 0 us -> 78.5 us
  matrix products: 92.2 us -> 24.7 us
  blocking collectives: 67.5 us -> 15.6 us
  other arithmetic: 32.6 us -> 6.31 us
  local copies, waits for them, and re-layouts: 18.8 us -> 11.7 us
    all_gather x2 -> x0, waiting for transfers between devices: 303 us -> none  [the longest x1 191 us: body(): value_piece = lax.all_gather(value_heads, 'ctx', axis=1, tiled=True)]
    reduce_scatter x1, waiting for transfers between devices: 52.3 us -> 149 us  [body(): lax.psum_scatter(partial_out.astype(jnp.bfloat16), 'head', scatter_dimens...]
    pallas_call x0 -> x1, Pallas kernels: none -> 78.5 us  [attend(): pl.pallas_call(attend_kernel, out_shape=jax.ShapeDtypeStruct((rows, HDIM)...]
    dot_general x21 -> x2, matrix products: 61.5 us -> 0.51 us  [the longest x1 0.3 us: live_lists(): live = jnp.dot(jnp.dot(pick, mask), pick.T)]
    all_to_all x2 -> x1, blocking collectives: 67.5 us -> 15.6 us  [body(): lax.all_to_all(attended.reshape(groups, tokens, HDIM), 'ctx', split_axis=...]
    convert_element_type x7 -> x0, other arithmetic: 31.3 us -> none  [the longest x6 29.4 us: one_head(): weights.astype(jnp.bfloat16)]
    all_to_all x2 -> x1, waiting for transfers between devices: 56.9 us -> 52.3 us  [body(): lax.all_to_all(jnp.stack(packs), 'ctx', split_axis=0, concat_axis=0, tile...]
  transfers between devices with their start and end apart: 6 -> 3, of which waited for: 6 -> 3; matrix products, arithmetic and copies ran while one was open for 4% -> 0% of each run, Pallas kernels for 0% -> 0%
where the time goes in v1:
time: 416 us; the launch traced here: 415 us
  waiting for transfers between devices  260 us (62%)
  Pallas kernels  78.5 us (19%)
  matrix products  24.7 us (6%)
  blocking collectives  15.6 us (4%)
  between operations  13.6 us (3%)
  local copies, waits for them, and re-layouts  11.7 us (3%)
  other arithmetic  6.31 us (2%)
  starting transfers between devices  5.24 us (1%)
    reduce_scatter x1, waiting for transfers between devices, body(): lax.psum_scatter(partial_out.astype(jnp.bfloat16), 'head', scatter_dimens...  149 us
    pallas_call x1, Pallas kernels, attend(): pl.pallas_call(attend_kernel, out_shape=jax.ShapeDtypeStruct((rows, HDIM)...  78.5 us
    all_gather x1, waiting for transfers between devices, body(): features = lax.all_gather(patch_rows, 'head', axis=1, tiled=True)  57.6 us
    all_to_all x1, waiting for transfers between devices, body(): lax.all_to_all(jnp.stack(packs), 'ctx', split_axis=0, concat_axis=0, tile...  52.3 us
    dot_general x3, matrix products, project(): jnp.dot(features, weight, preferred_element_type=jnp.float32)  16.3 us
    all_to_all x1, blocking collectives, body(): lax.all_to_all(attended.reshape(groups, tokens, HDIM), 'ctx', split_axis=...  15.6 us
  transfers between devices with their start and end apart: 3, of which 3 were waited for; matrix products, arithmetic and copies ran while one was open for 0% of the time, Pallas kernels for 0%

profile of v1, /device:TPU:1, one launch (start us, length us, event | category | flops | bytes accessed | tf_op | source)
XLA Modules:
  0.0 415.1 jit_solution(12700995406785552213)
XLA Ops:
  6.5 0.0 all-gather.2.cloned.1.call-start
  6.5 0.7 all-gather.2.cloned.1.call-update
  7.3 57.6 %all-gather.2.cloned.1.call-done = bf16[768,3072]{1,0:T(8,128)(2,1)} async-done(((bf16[768,768]{1,0:T(8,128)(2,1)}), bf16[768,3072]{1,0:T(8,128)(2,1)}) %all-gather.2.cloned.1.call-update) | async-done | bytes 4718608 | tf_op jit(solution)/shard_map/all_gather | solution.py:135
  64.8 0.0 copy-start.1
  64.8 0.0 copy-start.2
  64.8 7.8 %convolution_convert_fusion.1 = bf16[768,768]{0,1:T(8,128)(2,1)S(1)} fusion(bf16[768,3072]{1,0:T(8,128)(2,1)} %all-gather.2.cloned.1.call-done, bf16[3072,768]{1,0:T(8,128)(2,1)} %param.10), kind=kOutput, calls=%fused_computation.1 | convolution fusion | flops 3624468480 | bytes 10616832 | tf_op jit(solution)/shard_map/dot_general | solution.py:124
  72.6 0.0 slice-start
  72.6 0.1 fusion.30
  72.7 0.0 copy-done.1
  72.7 0.0 copy-done.2
  72.7 0.0 slice-start.1
  72.8 4.2 %convolution_convert_fusion.2 = bf16[768,768]{0,1:T(8,128)(2,1)S(1)} fusion(bf16[768,3072]{1,0:T(8,128)(2,1)S(1)} %copy-done.2, bf16[3072,768]{1,0:T(8,128)(2,1)S(1)} %copy-done.1), kind=kOutput, calls=%fused_computation.2 | convolution fusion | flops 3624468480 | bytes 10616832 | tf_op jit(solution)/shard_map/dot_general | solution.py:124
  76.9 0.0 slice-done
  76.9 0.0 slice-done.1
  77.0 4.4 %convolution_convert_fusion.3 = bf16[768,768]{0,1:T(8,128)(2,1)S(1)} fusion(bf16[768,3072]{1,0:T(8,128)(2,1)S(1)} %copy-done.2, bf16[3072,768]{1,0:T(8,128)(2,1)S(1)} %bitcast.65), kind=kOutput, calls=%fused_computation.3 | convolution fusion | flops 3624468480 | bytes 10616832 | tf_op jit(solution)/shard_map/dot_general | solution.py:124
  81.3 0.2 fusion.28
  81.5 0.9 fusion.5
  82.4 0.9 fusion.6
  83.3 0.9 fusion.7
  84.1 0.9 broadcast_dynamic-update-slice_fusion
  85.0 0.9 fusion.8
  85.9 0.9 fusion.9
  86.8 0.9 fusion.10
  87.7 0.9 broadcast_dynamic-update-slice_fusion.1
  88.6 0.0 copy-start.3
  88.6 0.0 copy-start.4
  88.6 5.2 %all-to-all-start = ((bf16[8,768,384]{1,2,0:T(8,128)(2,1)}), bf16[8,768,384]{1,2,0:T(8,128)(2,1)}, u32[]{:S(2)}, u32[]{:S(2)}) async-start(bf16[8,768,384]{1,2,0:T(8,128)(2,1)} %broadcast_dynamic-update-slice_fusion.1), calls=%async_computation | async-start | bytes 9437184 | tf_op jit(solution)/shard_map/all_to_all | solution.py:148
  93.8 0.0 reduce-scatter.2.cloned.1.call-start
  93.9 0.0 copy-done.3
  93.9 0.0 copy-done.4
  93.9 0.3 broadcast_compare_fusion
  94.2 0.2 fusion.1
  94.4 0.1 copy.14
  94.5 0.9 select_reduce_fusion
  95.3 0.1 slice_reduce_fusion
  95.4 0.1 fusion.17
  95.5 0.1 select_n.22.key_list
  95.6 0.1 select_n.24.value_list
  95.7 0.1 pad_add_fusion.counts
  95.8 52.3 %all-to-all-done = bf16[8,768,384]{1,2,0:T(8,128)(2,1)} async-done(((bf16[8,768,384]{1,2,0:T(8,128)(2,1)}), bf16[8,768,384]{1,2,0:T(8,128)(2,1)}, u32[]{:S(2)}, u32[]{:S(2)}) %all-to-all-start) | async-done | bytes 4718624 | tf_op jit(solution)/shard_map/all_to_all | solution.py:148
  148.1 6.7 %copy.15 = bf16[8,768,384]{2,1,0:T(8,128)(2,1)} copy(bf16[8,768,384]{1,2,0:T(8,128)(2,1)} %all-to-all-done) | data formatting | bytes 9437184 | tf_op jit(solution)/shard_map/all_to_all | solution.py:148
  154.8 0.0 copy-start
  154.8 2.3 copy-done
  157.1 78.5 %attend.1 = bf16[6144,128]{1,0:T(8,128)(2,1)S(1)} custom-call(s32[2304]{0:T(1024)S(1)} %select_n.22.key_list, s32[2304]{0:T(1024)S(1)} %select_n.24.value_list, s32[49]{0:T(128)S(1)} %pad_add_fusion.counts, bf16[6144,384]{1,0:T(8,128)(2,1)S(1)} %bitcast.62), custom_call_target="tpu_custom_call" | custom-call | flops 19327352832 | bytes 6291456 | tf_op jit(solution)/shard_map/attend/pallas_call | solution.py:83
  235.6 15.6 %all_to_all.10 = bf16[8,768,128]{2,1,0:T(8,128)(2,1)S(1)} all-to-all(bf16[8,768,128]{2,1,0:T(8,128)(2,1)S(1)} %bitcast.63), channel_id=1, replica_groups=mesh['ctx'=8,'head'=4,'dp'=4] {'ctx'}, dimensions={0} | all-to-all | bytes 3145728 | tf_op jit(solution)/shard_map/all_to_all | solution.py:150
  251.5 7.8 %convolution_convert_fusion = bf16[768,3072]{1,0:T(8,128)(2,1)} fusion(bf16[768,768]{1,0:T(8,128)(2,1)S(1)} %fusion.11, bf16[768,3072]{1,0:T(8,128)(2,1)} %param.11), kind=kOutput, calls=%fused_computation | convolution fusion | flops 3626237952 | bytes 10616832 | tf_op jit(solution)/shard_map/dot_general | solution.py:154
  259.3 0.0 reduce-scatter.2.cloned.1.call-update
  259.3 148.9 %reduce-scatter.2.cloned.1.call-done = bf16[768,768]{1,0:T(8,128)(2,1)} async-done(((bf16[768,3072]{1,0:T(8,128)(2,1)}), bf16[768,768]{1,0:T(8,128)(2,1)}) %reduce-scatter.2.cloned.1.call-update) | async-done | bytes 1179664 | tf_op jit(solution)/shard_map/reduce_scatter | solution.py:155
  (8 shorter events, 0.3 us)
Async XLA Ops:
  6.5 58.3 %all-gather.2.cloned.1.call-start = ((), (), s32[]{:S(2)}) async-start(), calls=%async_computation.3 | async-start | bytes 5898240 | tf_op jit(solution)/shard_map/all_gather | solution.py:135
  64.8 7.9 %copy-start.1 = (bf16[3072,768]{1,0:T(8,128)(2,1)S(1)}, bf16[3072,768]{1,0:T(8,128)(2,1)}, u32[]{:S(2)}) copy-start(bf16[3072,768]{1,0:T(8,128)(2,1)} %param.9) | copy-start | bytes 14155780
  64.8 7.9 %copy-start.2 = (bf16[768,3072]{1,0:T(8,128)(2,1)S(1)}, bf16[768,3072]{1,0:T(8,128)(2,1)}, u32[]{:S(2)}) copy-start(bf16[768,3072]{1,0:T(8,128)(2,1)} %all-gather.2.cloned.1.call-done) | copy-start | bytes 14155780
  72.6 4.3 %slice-start = ((s8[4718592]{0:T(1024)(128)(4,1)}), s8[4194304]{0:T(1024)(128)(4,1)S(1)}, s32[]{:S(2)}) async-start(s8[4718592]{0:T(1024)(128)(4,1)} %bitcast.64), calls=%async_computation.5 | async-start | bytes 8388608
  72.7 4.2 %slice-start.1 = ((s8[4718592]{0:T(1024)(128)(4,1)}), s8[524288]{0:T(1024)(128)(4,1)S(1)}, s32[]{:S(2)}) async-start(s8[4718592]{0:T(1024)(128)(4,1)} %bitcast.64), calls=%async_computation.6 | async-start | bytes 1048576
  88.6 5.3 %copy-start.3 = (s32[48,48]{1,0:T(8,128)S(1)}, s32[48,48]{1,0:T(8,128)}, u32[]{:S(2)}) copy-start(s32[48,48]{1,0:T(8,128)} %param.13) | copy-start | bytes 27652
  88.6 5.3 %copy-start.4 = (s32[48]{0:T(128)S(1)}, s32[48]{0:T(128)}, u32[]{:S(2)}) copy-start(s32[48]{0:T(128)} %param.12) | copy-start | bytes 580
  88.6 59.5 %all-to-all-start = ((bf16[8,768,384]{1,2,0:T(8,128)(2,1)}), bf16[8,768,384]{1,2,0:T(8,128)(2,1)}, u32[]{:S(2)}, u32[]{:S(2)}) async-start(bf16[8,768,384]{1,2,0:T(8,128)(2,1)} %broadcast_dynamic-update-slice_fusion.1), calls=%async_computation | async-start | bytes 9437184 | tf_op jit(solution)/shard_map/all_to_all | solution.py:148
  93.8 314.5 %reduce-scatter.2.cloned.1.call-start = ((), (), s32[]{:S(2)}) async-start(), calls=%async_computation.4 | async-start | bytes 5898240 | tf_op jit(solution)/shard_map/reduce_scatter | solution.py:155
  154.8 2.3 copy-start
Sparse Core Ops, SparseCore 0:
  9.0 55.7 all-gather.1
  259.4 148.7 reduce-scatter.1

commit v2 on v1

v2 whole, which is shorter than its diff:
```python
import functools
import math

import jax
import jax.numpy as jnp
from jax import lax
from jax.experimental import pallas as pl
from jax.experimental.pallas import tpu as pltpu
from jax.sharding import PartitionSpec as P

HDIM = 128
TILE = 128
GROUP = 8
TOGETHER = 3
FRONT_ROWS = 128
FRONT_AHEAD = 2
MESH = pl.DeviceIdType.MESH
LOG2E = 1.4426950408889634


def attend_kernel(
    order, key_list, value_list, counts, qkv_ref, out_ref, keys_t, values, scores
):
    tiles = qkv_ref.shape[0] // TILE
    pad = key_list.shape[0] // tiles
    stages = tiles // TOGETHER
    factor = LOG2E / math.sqrt(HDIM)

    def at(tile):
        return pl.ds(pl.multiple_of(tile * TILE, TILE), TILE)

    def score_step(queries, stage, g, peaks):
        fresh = []
        for j in range(TOGETHER):
            base = (stage * TOGETHER + j) * pad + g * GROUP
            peak = peaks[j]
            for i in range(0, GROUP, 2):
                block = jnp.concatenate(
                    [keys_t[:, at(key_list[base + i])], keys_t[:, at(key_list[base + i + 1])]], axis=1
                )
                found = jnp.dot(queries[j], block, preferred_element_type=jnp.float32)
                scores[lax.rem(stage, 2), g, j, :, i * TILE : (i + 2) * TILE] = found
                peak = jnp.maximum(peak, jnp.maximum(found[:, :TILE], found[:, TILE:]))
            fresh.append(peak)
        return tuple(fresh)

    def value_step(stage, g, row_peaks, totals):
        fresh = []
        for j in range(TOGETHER):
            base = (stage * TOGETHER + j) * pad + g * GROUP
            weight = jnp.exp2(
                scores[lax.rem(stage, 2), g, j] * factor - row_peaks[j]
            ).astype(jnp.bfloat16)
            block = jnp.concatenate([values[at(value_list[base + i]), :] for i in range(GROUP)], axis=0)
            fresh.append(totals[j] + jnp.dot(weight, block, preferred_element_type=jnp.float32))
        return tuple(fresh)

    def load_queries(stage):
        return [qkv_ref[at(order[stage * TOGETHER + j]), :HDIM] for j in range(TOGETHER)]

    def steps_of(stage):
        return (counts[stage * TOGETHER] + GROUP - 1) // GROUP

    def to_rows(peaks):
        return tuple(
            jnp.broadcast_to(jnp.max(peak, axis=1, keepdims=True) * factor, (TILE, 1)) for peak in peaks
        )

    def finish(stage, totals):
        for j in range(TOGETHER):
            out_ref[at(order[stage * TOGETHER + j]), :] = (
                totals[j][:, :HDIM] / totals[j][:, HDIM:]
            ).astype(jnp.bfloat16)

    low = tuple(jnp.full((TILE, TILE), -jnp.inf, jnp.float32) for _ in range(TOGETHER))
    zero = tuple(jnp.zeros((TILE, 2 * HDIM), jnp.float32) for _ in range(TOGETHER))

    @pl.when(counts[tiles] == 1)
    def _():
        def prepare(t, carry):
            keys_t[:, at(t)] = qkv_ref[at(t), HDIM : 2 * HDIM].T
            values[at(t), :HDIM] = qkv_ref[at(t), 2 * HDIM :]
            values[at(t), HDIM:] = jnp.ones((TILE, HDIM), jnp.bfloat16)
            return carry

        lax.fori_loop(0, tiles, prepare, 0, unroll=2)
        values[pl.ds(tiles * TILE, TILE), :] = jnp.zeros((TILE, 2 * HDIM), jnp.bfloat16)

        queries = load_queries(0)
        peaks = lax.fori_loop(0, steps_of(0), lambda g, p: score_step(queries, 0, g, p), low)

        def stage_body(stage, row_peaks):
            queries = load_queries(stage)

            def both(g, carry):
                peaks, totals = carry
                totals = value_step(stage - 1, g, row_peaks, totals)
                peaks = score_step(queries, stage, g, peaks)
                return peaks, totals

            peaks, totals = lax.fori_loop(0, steps_of(stage - 1), both, (low, zero))
            finish(stage - 1, totals)
            return to_rows(peaks)

        row_peaks = lax.fori_loop(1, stages, stage_body, to_rows(peaks))
        totals = lax.fori_loop(
            0, steps_of(stages - 1), lambda g, t: value_step(stages - 1, g, row_peaks, t), zero
        )
        finish(stages - 1, totals)


def attend(order, key_list, value_list, counts, qkv):
    rows = qkv.shape[0]
    return pl.pallas_call(
        attend_kernel,
        out_shape=jax.ShapeDtypeStruct((rows, HDIM), jnp.bfloat16),
        grid_spec=pltpu.PrefetchScalarGridSpec(
            num_scalar_prefetch=4,
            grid=(1,),
            in_specs=[pl.BlockSpec((rows, 3 * HDIM), lambda i, *_: (0, 0))],
            out_specs=pl.BlockSpec((rows, HDIM), lambda i, *_: (0, 0)),
            scratch_shapes=[
                pltpu.VMEM((HDIM, rows), jnp.bfloat16),
                pltpu.VMEM((rows + TILE, 2 * HDIM), jnp.bfloat16),
                pltpu.VMEM(
                    (2, rows // (TILE * GROUP), TOGETHER, TILE, GROUP * TILE), jnp.float32
                ),
            ],
        ),
        compiler_params=pltpu.CompilerParams(vmem_limit_bytes=52 * 1024 * 1024),
        cost_estimate=pl.CostEstimate(
            flops=4 * rows * rows * HDIM, bytes_accessed=8 * rows * HDIM, transcendentals=rows * rows
        ),
        name="attend",
    )(order, key_list, value_list, counts, qkv)


def live_lists(tile_slot, tile_mask, active):
    tiles = tile_slot.shape[0]
    places = jnp.arange(tiles, dtype=jnp.int32)
    pick = (tile_slot[:, None] == places[None, :]).astype(jnp.float32)
    mask = (tile_mask == 1).astype(jnp.float32)
    size = jnp.sum(mask, axis=1)
    ahead = (size[None, :] > size[:, None]) | (
        (size[None, :] == size[:, None]) & (places[None, :] < places[:, None])
    )
    position = jnp.sum(ahead.astype(jnp.int32), axis=1)
    arrange = (position[None, :] == places[:, None]).astype(jnp.float32)
    chosen = jnp.dot(arrange, pick.T)
    order = jnp.sum(chosen * places[None, :].astype(jnp.float32), axis=1).astype(jnp.int32)
    live = jnp.dot(jnp.dot(arrange, mask), pick.T)
    upper = (places[:, None] <= places[None, :]).astype(jnp.float32)
    rank = jnp.dot(live, upper).astype(jnp.int32) - 1
    counts = rank[:, -1] + 1
    hit = (rank[:, :, None] == places[None, None, :]) & (live[:, :, None] > 0.5)
    listed = jnp.sum(jnp.where(hit, places[None, :, None], 0), axis=1)
    used = places[None, :] < counts[:, None]
    key_list = jnp.where(used, listed, listed[:, :1]).reshape(-1)
    value_list = jnp.where(used, listed, tiles).reshape(-1)
    counts = jnp.concatenate([counts, active.astype(jnp.int32)[None]])
    return order, key_list, value_list, counts


def head_slot(head):
    return head + head // 3


def sync_peers(here, peers):
    barrier = pltpu.get_barrier_semaphore()
    for peer in peers:
        pl.semaphore_signal(barrier, inc=1, device_id=peer, device_id_type=MESH)
    pl.semaphore_wait(barrier, len(peers))


def whereabouts(groups, ring):
    ctx, head, part = lax.axis_index("ctx"), lax.axis_index("head"), lax.axis_index("dp")
    shift = lax.rem(part, 2)
    right, left = lax.rem(head + 1, ring), lax.rem(head + ring - 1, ring)
    peers = [(ctx, left, part), (ctx, right, part)]
    peers += [(lax.rem(ctx + i, groups), head, part) for i in range(1, groups)]
    active = lax.rem(ctx + groups - shift, 4) != 3
    return ctx, head, part, shift, right, left, peers, active


def front_kernel(
    groups, ring, heads, patch_ref, wq_ref, wk_ref, wv_ref, out_ref,
    rows_all, weights, stage, weight_sem, own_sem, left_sem, right_sem, pass_sem, far_sem,
    give_sem, self_sem, take_sem,
):
    tokens, width = patch_ref.shape
    chunk = FRONT_ROWS
    chunks = tokens // chunk
    ctx, head, part, shift, right, left, peers, active = whereabouts(groups, ring)
    across = lax.rem(head + 2, ring)

    loads = [
        pltpu.make_async_copy(ref, weights.at[i], weight_sem.at[i])
        for i, ref in enumerate((wq_ref, wk_ref, wv_ref))
    ]
    for load in loads:
        load.start()
    sync_peers(ctx, peers)

    def span(c):
        return pl.ds(pl.multiple_of(c * chunk, chunk), chunk)

    def own_copy(c, way, to, sems):
        return pltpu.make_async_remote_copy(
            src_ref=patch_ref.at[span(c), :],
            dst_ref=rows_all.at[head, span(c), :],
            send_sem=own_sem.at[way, c],
            recv_sem=sems.at[c],
            device_id=(ctx, to, part),
            device_id_type=MESH,
        )

    def arrival(slot, c, sems):
        return pltpu.make_async_copy(
            rows_all.at[slot, span(c), :], rows_all.at[slot, span(c), :], sems.at[c]
        )

    def send_own(c):
        own_copy(c, 0, right, left_sem).start()
        own_copy(c, 1, left, right_sem).start()

    def pass_copy(c, slot, to):
        return pltpu.make_async_remote_copy(
            src_ref=rows_all.at[slot, span(c), :],
            dst_ref=rows_all.at[slot, span(c), :],
            send_sem=pass_sem.at[c],
            recv_sem=far_sem.at[c],
            device_id=(ctx, to, part),
            device_id_type=MESH,
        )

    def give_copy(c, h):
        target = lax.rem(head_slot(h) + shift, groups)
        return target, pltpu.make_async_remote_copy(
            src_ref=stage.at[h, span(c), :],
            dst_ref=out_ref.at[ctx, span(c), :],
            send_sem=give_sem.at[h, c],
            recv_sem=take_sem,
            device_id=(target, head, part),
            device_id_type=MESH,
        )

    def keep_copy(c, h):
        return pltpu.make_async_copy(
            stage.at[h, span(c), :], out_ref.at[ctx, span(c), :], self_sem.at[c]
        )

    def project_chunk(c):
        for pair in range(heads // 2):
            cols = slice(pair * 2 * HDIM, (pair + 1) * 2 * HDIM)
            for i in range(3):
                total = jnp.dot(
                    rows_all[0, span(c), :], weights[i, :width, cols],
                    preferred_element_type=jnp.float32,
                )
                for k in range(1, ring):
                    total += jnp.dot(
                        rows_all[k, span(c), :], weights[i, k * width : (k + 1) * width, cols],
                        preferred_element_type=jnp.float32,
                    )
                total = total.astype(jnp.bfloat16)
                for j in range(2):
                    stage[2 * pair + j, span(c), i * HDIM : (i + 1) * HDIM] = total[
                        :, j * HDIM : (j + 1) * HDIM
                    ]
            for j in range(2):
                h = 2 * pair + j
                target, copy = give_copy(c, h)

                @pl.when(target != ctx)
                def _():
                    copy.start()

                @pl.when(target == ctx)
                def _():
                    keep_copy(c, h).start()

    ahead = min(FRONT_AHEAD, chunks)
    for c in range(ahead):
        send_own(c)
    rows_all[head] = patch_ref[...]
    for load in loads:
        load.wait()

    def step(c, carry):
        @pl.when(c < chunks)
        def _():
            arrival(left, c, left_sem).wait()
            arrival(right, c, right_sem).wait()

            @pl.when(lax.rem(c, 2) == 0)
            def _():
                pass_copy(c, left, right).start()

            @pl.when(lax.rem(c, 2) == 1)
            def _():
                pass_copy(c, right, left).start()

        @pl.when(c + ahead < chunks)
        def _():
            send_own(c + ahead)

        @pl.when(c > 0)
        def _():
            arrival(across, c - 1, far_sem).wait()
            project_chunk(c - 1)

        return carry

    lax.fori_loop(0, chunks + 1, step, 0)

    def settle(c, carry):
        own_copy(c, 0, right, left_sem).wait_send()
        own_copy(c, 1, left, right_sem).wait_send()
        pass_copy(c, left, right).wait_send()
        for h in range(heads):
            target, copy = give_copy(c, h)

            @pl.when(target != ctx)
            def _():
                copy.wait_send()

            @pl.when(target == ctx)
            def _():
                keep_copy(c, h).wait()

        return carry

    lax.fori_loop(0, chunks, settle, 0)

    @pl.when(active)
    def _():
        others = pl.ds(0, groups - 1)
        pltpu.make_async_copy(out_ref.at[others], out_ref.at[others], take_sem).wait()


def front(groups, ring, patch_rows, query_weight, key_weight, value_weight):
    tokens, width = patch_rows.shape
    depth, columns = query_weight.shape
    heads = columns // HDIM
    chunks = tokens // FRONT_ROWS
    dma = pltpu.SemaphoreType.DMA
    return pl.pallas_call(
        functools.partial(front_kernel, groups, ring, heads),
        out_shape=jax.ShapeDtypeStruct((groups, tokens, 3 * HDIM), jnp.bfloat16),
        in_specs=[pl.BlockSpec(memory_space=pltpu.VMEM)] + [pl.BlockSpec(memory_space=pl.ANY)] * 3,
        out_specs=pl.BlockSpec(memory_space=pl.ANY),
        scratch_shapes=[
            pltpu.VMEM((ring, tokens, width), jnp.bfloat16),
            pltpu.VMEM((3, depth, columns), jnp.bfloat16),
            pltpu.VMEM((heads, tokens, 3 * HDIM), jnp.bfloat16),
            dma((3,)),
            dma((2, chunks)),
            dma((chunks,)),
            dma((chunks,)),
            dma((chunks,)),
            dma((chunks,)),
            dma((heads, chunks)),
            dma((chunks,)),
            dma,
        ],
        compiler_params=pltpu.CompilerParams(
            collective_id=0, has_side_effects=True, vmem_limit_bytes=40 * 1024 * 1024
        ),
        cost_estimate=pl.CostEstimate(
            flops=6 * tokens * depth * columns, bytes_accessed=8 * depth * columns, transcendentals=0
        ),
        name="front",
    )(patch_rows, query_weight, key_weight, value_weight)


def body(patch_rows, query_weight, key_weight, value_weight, output_weight, tile_slot, tile_mask):
    groups = lax.axis_size("ctx")
    shard = lax.axis_index("ctx")
    tokens = patch_rows.shape[0]
    ring = lax.axis_size("head")
    heads = query_weight.shape[1] // HDIM
    shift = lax.rem(lax.axis_index("dp"), 2)
    active = lax.rem(shard + groups - shift, 4) != 3
    order, key_list, value_list, counts = live_lists(tile_slot, tile_mask, active)
    sent = front(groups, ring, patch_rows, query_weight, key_weight, value_weight)
    attended = attend(order, key_list, value_list, counts, sent.reshape(groups * tokens, 3 * HDIM))
    back = lax.all_to_all(
        attended.reshape(groups, tokens, HDIM), "ctx", split_axis=0, concat_axis=0, tiled=True
    )
    back = jnp.roll(back, -shift, axis=0)
    attended = jnp.concatenate([back[head_slot(h)] for h in range(heads)], axis=1)
    partial_out = jnp.dot(attended, output_weight, preferred_element_type=jnp.float32)
    return lax.psum_scatter(
        partial_out.astype(jnp.bfloat16), "head", scatter_dimension=1, tiled=True
    )


def solution(mesh):
    in_specs = (
        P(("dp", "ctx"), "head"),
        P(None, "head"),
        P(None, "head"),
        P(None, "head"),
        P("head", None),
        P("dp"),
        P("dp", None),
    )
    out_specs = P(("dp", "ctx"), "head")
    return jax.shard_map(body, mesh=mesh, in_specs=in_specs, out_specs=out_specs, check_vma=False)
```

time: 416 us -> 223 us (0.54)
  waiting for transfers between devices: 260 us -> 74.5 us
  starting transfers between devices: 5.24 us -> 37.6 us
  matrix products: 24.7 us -> 7.45 us
  blocking collectives: 15.6 us -> 0 us
    reduce_scatter x1, waiting for transfers between devices: 149 us -> 54.6 us  [body(): lax.psum_scatter(partial_out.astype(jnp.bfloat16), 'head', scatter_dimens...]
    pallas_call x0 -> x1, Pallas kernels: none -> 75 us  [front(): pl.pallas_call(functools.partial(front_kernel, groups, ring, heads), out_...]
    pallas_call x1, Pallas kernels: 78.5 us -> 4.35 us  [attend(): pl.pallas_call(attend_kernel, out_shape=jax.ShapeDtypeStruct((rows, HDIM)...]
    all_gather x1 -> x0, waiting for transfers between devices: 57.6 us -> none  [body(): features = lax.all_gather(patch_rows, 'head', axis=1, tiled=True)]
    all_to_all x1, waiting for transfers between devices: 52.3 us -> 19.8 us  [body(): lax.all_to_all(attended.reshape(groups, tokens, HDIM), 'ctx', split_axis=...]
    all_to_all x1, starting transfers between devices: 5.2 us -> 37.6 us  [body(): lax.all_to_all(attended.reshape(groups, tokens, HDIM), 'ctx', split_axis=...]
    all_to_all x1 -> x0, blocking collectives: 15.6 us -> none  [body(): lax.all_to_all(attended.reshape(groups, tokens, HDIM), 'ctx', split_axis=...]
    dot_general x4 -> x2, matrix products: 16.6 us -> 1.76 us  [the longest x1 0.9 us: live_lists(): live = jnp.dot(jnp.dot(arrange, mask), pick.T)]
  transfers between devices with their start and end apart: 3 -> 2, of which waited for: 3 -> 2; matrix products, arithmetic and copies ran while one was open for 0% -> 0% of each run, Pallas kernels for 0% -> 0%
where the time goes in v2:
time: 223 us
  Pallas kernels  79.4 us (36%)
  waiting for transfers between devices  74.5 us (33%)
  starting transfers between devices  37.6 us (17%)
  between operations  13.5 us (6%)
  local copies, waits for them, and re-layouts  7.78 us (3%)
  matrix products  7.45 us (3%)
  other arithmetic  2.63 us (1%)
    pallas_call x1, Pallas kernels, front(): pl.pallas_call(functools.partial(front_kernel, groups, ring, heads), out_...  75 us
    reduce_scatter x1, waiting for transfers between devices, body(): lax.psum_scatter(partial_out.astype(jnp.bfloat16), 'head', scatter_dimens...  54.6 us
    all_to_all x1, starting transfers between devices, body(): lax.all_to_all(attended.reshape(groups, tokens, HDIM), 'ctx', split_axis=...  37.6 us
    all_to_all x1, waiting for transfers between devices, body(): lax.all_to_all(attended.reshape(groups, tokens, HDIM), 'ctx', split_axis=...  19.8 us
    unnamed x13, local copies, waits for them, and re-layouts  7.4 us
    dot_general x1, matrix products, body(): jnp.dot(attended, output_weight, preferred_element_type=jnp.float32)  5.48 us
  transfers between devices with their start and end apart: 2, of which 2 were waited for; matrix products, arithmetic and copies ran while one was open for 0% of the time, Pallas kernels for 0%

profile of v2, /device:TPU:1, one launch (start us, length us, event | category | flops | bytes accessed | tf_op | source)
XLA Modules:
  0.0 222.9 jit_solution(9907419313086901900)
XLA Ops:
  6.5 0.8 convert_reduce_fusion.1
  7.4 0.2 convert_reduce_fusion
  7.6 0.9 broadcast_compare_fusion
  8.5 0.2 fusion.2
  8.7 0.1 copy.11
  8.8 0.9 fusion.6
  9.7 0.9 select_reduce_fusion
  10.5 0.1 slice_reduce_fusion
  10.6 0.1 pad_add_fusion.counts
  10.7 0.1 fusion.13
  10.8 0.1 select_n.37.value_list
  10.9 0.1 select_n.35.key_list
  10.9 0.0 copy-start
  10.9 2.3 %copy-done = bf16[3072,768]{1,0:T(8,128)(2,1)S(1)} copy-done((bf16[3072,768]{1,0:T(8,128)(2,1)S(1)}, bf16[3072,768]{1,0:T(8,128)(2,1)}, u32[]{:S(2)}) %copy-start) | copy-done | bytes 4718616
  13.3 0.0 copy-start.1
  13.3 1.3 copy-done.1
  14.6 75.0 %front.1 = bf16[8,768,384]{2,1,0:T(8,128)(2,1)S(1)} custom-call(bf16[768,768]{1,0:T(8,128)(2,1)S(1)} %copy-done.1, bf16[3072,768]{1,0:T(8,128)(2,1)S(1)} %copy-done, bf16[3072,768]{1,0:T(8,128)(2,1)} %wk_ref.1, bf16[3072,768]{1,0:T(8,128)(2,1)} %wv_ref.1), custom_call_target="tpu_custom_call" | custom-call | flops 10871635968 | bytes 18874368 | tf_op jit(solution)/shard_map/front/pallas_call | solution.py:347
  89.6 0.0 copy-start.2
  89.6 2.1 copy-done.2
  91.7 4.4 %attend.1 = bf16[6144,128]{1,0:T(8,128)(2,1)} custom-call(s32[48]{0:T(128)S(1)} %convert_element_type.30.order, s32[2304]{0:T(1024)S(1)} %select_n.35.key_list, s32[2304]{0:T(1024)S(1)} %select_n.37.value_list, s32[49]{0:T(128)S(1)} %pad_add_fusion.counts, bf16[6144,384]{1,0:T(8,128)(2,1)} %bitcast.33), custom_call_target="tpu_custom_call" | custom-call | flops 19327352832 | bytes 6291456 | tf_op jit(solution)/shard_map/attend/pallas_call | solution.py:114
  96.1 37.6 %all-to-all-start = ((bf16[8,768,128]{2,1,0:T(8,128)(2,1)}), bf16[8,768,128]{2,1,0:T(8,128)(2,1)S(1)}, u32[]{:S(2)}, u32[]{:S(2)}) async-start(bf16[8,768,128]{2,1,0:T(8,128)(2,1)} %bitcast.3), calls=%async_computation | async-start | bytes 3145728 | tf_op jit(solution)/shard_map/all_to_all | solution.py:387
  133.7 0.0 reduce-scatter.2.cloned.1.call-start
  133.8 19.8 %all-to-all-done = bf16[8,768,128]{2,1,0:T(8,128)(2,1)S(1)} async-done(((bf16[8,768,128]{2,1,0:T(8,128)(2,1)}), bf16[8,768,128]{2,1,0:T(8,128)(2,1)S(1)}, u32[]{:S(2)}, u32[]{:S(2)}) %all-to-all-start) | async-done | bytes 1572896 | tf_op jit(solution)/shard_map/all_to_all | solution.py:387
  153.6 0.0 copy-start.3
  153.6 0.6 fusion
  154.5 1.4 copy-done.3
  155.9 5.5 %convolution_convert_fusion = bf16[768,3072]{1,0:T(8,128)(2,1)} fusion(bf16[768,768]{1,0:T(8,128)(2,1)S(1)} %fusion.7, bf16[768,3072]{1,0:T(8,128)(2,1)S(1)} %copy-done.3), kind=kOutput, calls=%fused_computation | convolution fusion | flops 3626237952 | bytes 10616832 | tf_op jit(solution)/shard_map/dot_general | solution.py:392
  161.4 0.0 reduce-scatter.2.cloned.1.call-update
  161.4 54.6 %reduce-scatter.2.cloned.1.call-done = bf16[768,768]{1,0:T(8,128)(2,1)} async-done(((bf16[768,3072]{1,0:T(8,128)(2,1)}), bf16[768,768]{1,0:T(8,128)(2,1)}) %reduce-scatter.2.cloned.1.call-update) | async-done | bytes 1179664 | tf_op jit(solution)/shard_map/reduce_scatter | solution.py:393
  (9 shorter events, 0.3 us)
Async XLA Ops:
  10.9 2.3 %copy-start = (bf16[3072,768]{1,0:T(8,128)(2,1)S(1)}, bf16[3072,768]{1,0:T(8,128)(2,1)}, u32[]{:S(2)}) copy-start(bf16[3072,768]{1,0:T(8,128)(2,1)} %wq_ref.1) | copy-start | bytes 14155780
  13.3 1.3 copy-start.1
  89.6 2.1 copy-start.2
  96.1 57.5 %all-to-all-start = ((bf16[8,768,128]{2,1,0:T(8,128)(2,1)}), bf16[8,768,128]{2,1,0:T(8,128)(2,1)S(1)}, u32[]{:S(2)}, u32[]{:S(2)}) async-start(bf16[8,768,128]{2,1,0:T(8,128)(2,1)} %bitcast.3), calls=%async_computation | async-start | bytes 3145728 | tf_op jit(solution)/shard_map/all_to_all | solution.py:387
  133.7 82.4 %reduce-scatter.2.cloned.1.call-start = ((), (), s32[]{:S(2)}) async-start(), calls=%async_computation.2 | async-start | bytes 5898240 | tf_op jit(solution)/shard_map/reduce_scatter | solution.py:393
  153.6 2.3 %copy-start.3 = (bf16[768,3072]{1,0:T(8,128)(2,1)S(1)}, bf16[768,3072]{1,0:T(8,128)(2,1)}, u32[]{:S(2)}) copy-start(bf16[768,3072]{1,0:T(8,128)(2,1)} %param.11) | copy-start | bytes 14155780
Sparse Core Ops, SparseCore 0:
  161.5 54.4 reduce-scatter.1

commit v3 on v2

--- a/solution.py
+++ b/solution.py
@@ -14,6 +14,7 @@
 TOGETHER = 3
 FRONT_ROWS = 128
 FRONT_AHEAD = 2
+BACK_ROWS = 128
 MESH = pl.DeviceIdType.MESH
 LOG2E = 1.4426950408889634
 
@@ -373,6 +374,218 @@
     )(patch_rows, query_weight, key_weight, value_weight)
 
 
+def back_kernel(
+    groups, ring, heads, att_ref, wo_ref, out_ref,
+    gathered, weights, far_out, far_in, side_out, side_in, own, pending,
+    weight_sem, give_sem, self_sem, take_sem, far_send, far_recv, side_send, side_recv,
+):
+    tokens, width = out_ref.shape
+    chunk = BACK_ROWS
+    chunks = tokens // chunk
+    ctx, head, part, shift, right, left, peers, active = whereabouts(groups, ring)
+    across = lax.rem(head + 2, ring)
+    unit = lax.rem(ctx + groups - shift, groups)
+    mine = jnp.minimum(unit - unit // 4, heads - 1)
+
+    loads = [
+        pltpu.make_async_copy(
+            wo_ref.at[:, pl.ds(pl.multiple_of(block * width, width), width)],
+            weights.at[i],
+            weight_sem.at[i],
+        )
+        for i, block in enumerate((across, right, left, head))
+    ]
+    for load in loads:
+        load.start()
+    sync_peers(ctx, peers)
+
+    def span(c):
+        return pl.ds(pl.multiple_of(c * chunk, chunk), chunk)
+
+    def give_copy(c, i):
+        source = lax.rem(ctx + i, groups)
+        return pltpu.make_async_remote_copy(
+            src_ref=att_ref.at[source, span(c), :],
+            dst_ref=gathered.at[mine, span(c), :],
+            send_sem=give_sem.at[i - 1, c],
+            recv_sem=take_sem.at[c],
+            device_id=(source, head, part),
+            device_id_type=MESH,
+        )
+
+    def keep_copy(c):
+        return pltpu.make_async_copy(
+            att_ref.at[ctx, span(c), :], gathered.at[mine, span(c), :], self_sem.at[c]
+        )
+
+    @pl.when(active)
+    def _():
+        def give(c, carry):
+            keep_copy(c).start()
+            for i in range(1, groups):
+                give_copy(c, i).start()
+            return carry
+
+        lax.fori_loop(0, chunks, give, 0)
+
+    def far_copy(c, to):
+        return pltpu.make_async_remote_copy(
+            src_ref=far_out.at[span(c), :],
+            dst_ref=far_in.at[span(c), :],
+            send_sem=far_send.at[c],
+            recv_sem=far_recv.at[c],
+            device_id=(ctx, to, part),
+            device_id_type=MESH,
+        )
+
+    def side_copy(c, way, to):
+        return pltpu.make_async_remote_copy(
+            src_ref=side_out.at[way, span(c), :],
+            dst_ref=side_in.at[way, span(c), :],
+            send_sem=side_send.at[way, c],
+            recv_sem=side_recv.at[way, c],
+            device_id=(ctx, to, part),
+            device_id_type=MESH,
+        )
+
+    for load in loads:
+        load.wait()
+
+    def mix(c):
+        @pl.when(active)
+        def _():
+            keep_copy(c).wait()
+            others = pl.ds(0, heads - 1)
+            pltpu.make_async_copy(
+                gathered.at[others, span(c), :], gathered.at[others, span(c), :], take_sem.at[c]
+            ).wait()
+
+        @pl.when(jnp.logical_not(active))
+        def _():
+            pltpu.make_async_copy(
+                gathered.at[:, span(c), :], gathered.at[:, span(c), :], take_sem.at[c]
+            ).wait()
+
+        rows = jnp.concatenate([gathered[h, span(c), :] for h in range(heads)], axis=1)
+
+        def part_sum(i):
+            return jnp.dot(rows, weights[i], preferred_element_type=jnp.float32)
+
+        far_out[span(c), :] = part_sum(0).astype(jnp.bfloat16)
+        even = lax.rem(c, 2) == 0
+
+        @pl.when(even)
+        def _():
+            far_copy(c, right).start()
+            side_out[1, span(c), :] = part_sum(2).astype(jnp.bfloat16)
+            side_copy(c, 1, left).start()
+            pending[span(c), :] = part_sum(1)
+
+        @pl.when(jnp.logical_not(even))
+        def _():
+            far_copy(c, left).start()
+            side_out[0, span(c), :] = part_sum(1).astype(jnp.bfloat16)
+            side_copy(c, 0, right).start()
+            pending[span(c), :] = part_sum(2)
+
+        own[span(c), :] = part_sum(3)
+
+    def merge(c):
+        far_copy(c, right).wait_recv()
+        merged = (pending[span(c), :] + far_in[span(c), :].astype(jnp.float32)).astype(jnp.bfloat16)
+        even = lax.rem(c, 2) == 0
+
+        @pl.when(even)
+        def _():
+            side_out[0, span(c), :] = merged
+            side_copy(c, 0, right).start()
+
+        @pl.when(jnp.logical_not(even))
+        def _():
+            side_out[1, span(c), :] = merged
+            side_copy(c, 1, left).start()
+
+    def close(c):
+        side_copy(c, 0, right).wait_recv()
+        side_copy(c, 1, left).wait_recv()
+        out_ref[span(c), :] = (
+            own[span(c), :]
+            + side_in[0, span(c), :].astype(jnp.float32)
+            + side_in[1, span(c), :].astype(jnp.float32)
+        ).astype(jnp.bfloat16)
+
+    def step(c, carry):
+        @pl.when((c > 0) & (c <= chunks))
+        def _():
+            merge(c - 1)
+
+        @pl.when(c < chunks)
+        def _():
+            mix(c)
+
+        @pl.when(c > 1)
+        def _():
+            close(c - 2)
+
+        return carry
+
+    lax.fori_loop(0, chunks + 2, step, 0)
+
+    def settle(c, carry):
+        far_copy(c, right).wait_send()
+        side_copy(c, 0, right).wait_send()
+        side_copy(c, 1, left).wait_send()
+
+        @pl.when(active)
+        def _():
+            for i in range(1, groups):
+                give_copy(c, i).wait_send()
+
+        return carry
+
+    lax.fori_loop(0, chunks, settle, 0)
+
+
+def back(groups, ring, attended, output_weight):
+    tokens = attended.shape[1]
+    columns, depth = output_weight.shape
+    width = depth // ring
+    heads = columns // HDIM
+    chunks = tokens // BACK_ROWS
+    dma = pltpu.SemaphoreType.DMA
+    return pl.pallas_call(
+        functools.partial(back_kernel, groups, ring, heads),
+        out_shape=jax.ShapeDtypeStruct((tokens, width), jnp.bfloat16),
+        in_specs=[pl.BlockSpec(memory_space=pl.ANY)] * 2,
+        out_specs=pl.BlockSpec(memory_space=pltpu.VMEM),
+        scratch_shapes=[
+            pltpu.VMEM((heads, tokens, HDIM), jnp.bfloat16),
+            pltpu.VMEM((ring, columns, width), jnp.bfloat16),
+            pltpu.VMEM((tokens, width), jnp.bfloat16),
+            pltpu.VMEM((tokens, width), jnp.bfloat16),
+            pltpu.VMEM((2, tokens, width), jnp.bfloat16),
+            pltpu.VMEM((2, tokens, width), jnp.bfloat16),
+            pltpu.VMEM((tokens, width), jnp.float32),
+            pltpu.VMEM((tokens, width), jnp.float32),
+            dma((ring,)),
+            dma((groups - 1, chunks)),
+            dma((chunks,)),
+            dma((chunks,)),
+            dma((chunks,)),
+            dma((chunks,)),
+            dma((2, chunks)),
+            dma((2, chunks)),
+        ],
+        compiler_params=pltpu.CompilerParams(
+            collective_id=1, has_side_effects=True, vmem_limit_bytes=40 * 1024 * 1024
+        ),
+        cost_estimate=pl.CostEstimate(
+            flops=2 * tokens * depth * columns, bytes_accessed=2 * depth * columns, transcendentals=0
+        ),
+        name="back",
+    )(attended, output_weight)
+
+
 def body(patch_rows, query_weight, key_weight, value_weight, output_weight, tile_slot, tile_mask):
     groups = lax.axis_size("ctx")
     shard = lax.axis_index("ctx")
@@ -384,15 +597,7 @@
     order, key_list, value_list, counts = live_lists(tile_slot, tile_mask, active)
     sent = front(groups, ring, patch_rows, query_weight, key_weight, value_weight)
     attended = attend(order, key_list, value_list, counts, sent.reshape(groups * tokens, 3 * HDIM))
-    back = lax.all_to_all(
-        attended.reshape(groups, tokens, HDIM), "ctx", split_axis=0, concat_axis=0, tiled=True
-    )
-    back = jnp.roll(back, -shift, axis=0)
-    attended = jnp.concatenate([back[head_slot(h)] for h in range(heads)], axis=1)
-    partial_out = jnp.dot(attended, output_weight, preferred_element_type=jnp.float32)
-    return lax.psum_scatter(
-        partial_out.astype(jnp.bfloat16), "head", scatter_dimension=1, tiled=True
-    )
+    return back(groups, ring, attended.reshape(groups, tokens, HDIM), output_weight)
 
 
 def solution(mesh):

time: 223 us -> 186 us (0.83)
  the two profiles are of different devices: /device:TPU:1 before, /device:TPU:21 now
where the time goes in v3:
time: 186 us; the launch traced here: 185 us
  Pallas kernels  174 us (94%)
  local copies, waits for them, and re-layouts  7.08 us (4%)
  other arithmetic  2.07 us (1%)
  matrix products  1.96 us (1%)
    pallas_call x1, Pallas kernels, back(): pl.pallas_call(functools.partial(back_kernel, groups, ring, heads), out_s...  99.2 us
    pallas_call x1, Pallas kernels, front(): pl.pallas_call(functools.partial(front_kernel, groups, ring, heads), out_...  72 us
    unnamed x11, local copies, waits for them, and re-layouts  6.75 us

profile of v3, /device:TPU:21, one launch (start us, length us, event | category | flops | bytes accessed | tf_op | source)
XLA Modules:
  0.0 185.5 jit_solution(9754568690247453266)
XLA Ops:
  0.0 0.8 convert_reduce_fusion.1
  0.9 0.2 convert_reduce_fusion
  1.0 0.9 fusion.5
  1.9 0.9 broadcast_compare_fusion
  2.8 0.2 fusion.1
  3.0 0.1 copy.11
  3.1 0.9 select_reduce_fusion
  4.0 0.1 pad_add_fusion.counts
  4.1 0.1 slice_reduce_fusion
  4.2 0.1 fusion.6
  4.3 0.1 select_n.24.value_list
  4.3 0.1 select_n.22.key_list
  4.4 0.0 copy-start
  4.4 2.3 %copy-done = bf16[3072,768]{1,0:T(8,128)(2,1)S(1)} copy-done((bf16[3072,768]{1,0:T(8,128)(2,1)S(1)}, bf16[3072,768]{1,0:T(8,128)(2,1)}, u32[]{:S(2)}) %copy-start) | copy-done | bytes 4718616
  6.7 0.0 copy-start.1
  6.7 1.3 copy-done.1
  8.0 0.0 slice-start
  8.0 72.0 %front.1 = bf16[8,768,384]{2,1,0:T(8,128)(2,1)S(1)} custom-call(bf16[768,768]{1,0:T(8,128)(2,1)S(1)} %copy-done.1, bf16[3072,768]{1,0:T(8,128)(2,1)S(1)} %copy-done, bf16[3072,768]{1,0:T(8,128)(2,1)} %wk_ref.1, bf16[3072,768]{1,0:T(8,128)(2,1)} %wv_ref.1), custom_call_target="tpu_custom_call" | custom-call | flops 10871635968 | bytes 18874368 | tf_op jit(solution)/shard_map/front/pallas_call | solution.py:348
  80.0 0.0 copy-start.2
  80.0 2.1 %copy-done.2 = bf16[8,768,384]{2,1,0:T(8,128)(2,1)} copy-done((bf16[8,768,384]{2,1,0:T(8,128)(2,1)}, bf16[8,768,384]{2,1,0:T(8,128)(2,1)S(1)}, u32[]{:S(2)}) %copy-start.2) | copy-done | bytes 4718616
  82.1 0.0 slice-start.1
  82.1 3.2 %attend.1 = bf16[6144,128]{1,0:T(8,128)(2,1)S(1)} custom-call(s32[48]{0:T(128)S(1)} %convert_element_type.27.order, s32[2304]{0:T(1024)S(1)} %select_n.22.key_list, s32[2304]{0:T(1024)S(1)} %select_n.24.value_list, s32[49]{0:T(128)S(1)} %pad_add_fusion.counts, bf16[6144,384]{1,0:T(8,128)(2,1)} %bitcast.9), custom_call_target="tpu_custom_call" | custom-call | flops 19327352832 | bytes 6291456 | tf_op jit(solution)/shard_map/attend/pallas_call | solution.py:115
  85.3 0.0 slice-done
  85.3 0.0 slice-done.1
  85.3 99.2 %back.1 = bf16[768,768]{1,0:T(8,128)(2,1)S(1)} custom-call(bf16[8,768,128]{2,1,0:T(8,128)(2,1)S(1)} %bitcast.10, bf16[768,3072]{1,0:T(8,128)(2,1)S(1)} %bitcast.8), custom_call_target="tpu_custom_call" | custom-call | flops 3623878656 | bytes 4718592 | tf_op jit(solution)/shard_map/back/pallas_call | solution.py:556
  184.5 1.0 copy.13
  (4 shorter events, 0.0 us)
Async XLA Ops:
  4.4 2.3 %copy-start = (bf16[3072,768]{1,0:T(8,128)(2,1)S(1)}, bf16[3072,768]{1,0:T(8,128)(2,1)}, u32[]{:S(2)}) copy-start(bf16[3072,768]{1,0:T(8,128)(2,1)} %wq_ref.1) | copy-start | bytes 14155780
  6.7 1.3 copy-start.1
  8.0 77.3 %slice-start = ((s8[4718592]{0:T(1024)(128)(4,1)}), s8[4194304]{0:T(1024)(128)(4,1)S(1)}, s32[]{:S(2)}) async-start(s8[4718592]{0:T(1024)(128)(4,1)} %bitcast.7), calls=%async_computation | async-start | bytes 8388608
  80.0 2.1 %copy-start.2 = (bf16[8,768,384]{2,1,0:T(8,128)(2,1)}, bf16[8,768,384]{2,1,0:T(8,128)(2,1)S(1)}, u32[]{:S(2)}) copy-start(bf16[8,768,384]{2,1,0:T(8,128)(2,1)S(1)} %front.1) | copy-start | bytes 14155780
  82.1 3.2 %slice-start.1 = ((s8[4718592]{0:T(1024)(128)(4,1)}), s8[524288]{0:T(1024)(128)(4,1)S(1)}, s32[]{:S(2)}) async-start(s8[4718592]{0:T(1024)(128)(4,1)} %bitcast.7), calls=%async_computation.1 | async-start | bytes 1048576

commit v4 on v3

--- a/solution.py
+++ b/solution.py
@@ -12,6 +12,7 @@
 TILE = 128
 GROUP = 8
 TOGETHER = 3
+WIDE = 2
 FRONT_ROWS = 128
 FRONT_AHEAD = 2
 BACK_ROWS = 128
@@ -20,72 +21,116 @@
 
 
 def attend_kernel(
-    order, key_list, value_list, counts, qkv_ref, out_ref, keys_t, values, scores
+    is_active, slot_ref, mask_ref, qkv_ref, out_ref,
+    query_key, values, scores, plan_rows, plan, load_sem, plan_sem,
 ):
-    tiles = qkv_ref.shape[0] // TILE
-    pad = key_list.shape[0] // tiles
+    tokens = out_ref.shape[0]
+    tiles = tokens // TILE
     stages = tiles // TOGETHER
     factor = LOG2E / math.sqrt(HDIM)
 
     def at(tile):
         return pl.ds(pl.multiple_of(tile * TILE, TILE), TILE)
+
+    def make_plan():
+        def iota(shape, axis):
+            return lax.broadcasted_iota(jnp.int32, shape, axis)
+
+        def product(a, b, dims=((1,), (0,))):
+            return lax.dot_general(a, b, (dims, ((), ())), preferred_element_type=jnp.float32)
+
+        square = (tiles, tiles)
+        row, col = iota(square, 0), iota(square, 1)
+        home = (slot_ref[...] == row).astype(jnp.float32)
+        mask = (mask_ref[...] == 1).astype(jnp.float32)
+        size = jnp.sum(mask, axis=1, keepdims=True)
+        size_row = product(jnp.ones((1, tiles), jnp.float32), mask, ((1,), (1,)))
+        ahead = (size > size_row) | ((size == size_row) & (row < col))
+        position = jnp.sum(ahead.astype(jnp.float32), axis=0, keepdims=True)
+        arrange = (position == row.astype(jnp.float32)).astype(jnp.float32)
+        chosen = product(arrange, home)
+        order = jnp.sum(chosen * col.astype(jnp.float32), axis=1, keepdims=True)
+        live = product(product(arrange, mask), home)
+        rank = product(live, (row <= col).astype(jnp.float32))
+        count = jnp.sum(live, axis=1, keepdims=True)
+        rank = jnp.where(live > 0.5, rank - 1.0, -1.0)
+        lane = iota((tiles, 128), 1).astype(jnp.float32)
+        listed = jnp.zeros((tiles, 128), jnp.float32)
+        for u in range(1, tiles):
+            listed += jnp.where(rank[:, u : u + 1] == lane, float(u), 0.0)
+        used = lane < count
+        plan_rows[0] = jnp.where(used, listed, listed[:, :1]).astype(jnp.int32)
+        plan_rows[1] = jnp.where(used, listed, float(tiles)).astype(jnp.int32)
+        plan_rows[2] = jnp.where(lane == 0.0, order, count).astype(jnp.int32)
+        move = pltpu.make_async_copy(plan_rows, plan, plan_sem)
+        move.start()
+        move.wait()
 
     def score_step(queries, stage, g, peaks):
         fresh = []
         for j in range(TOGETHER):
-            base = (stage * TOGETHER + j) * pad + g * GROUP
+            r, base = stage * TOGETHER + j, g * GROUP
             peak = peaks[j]
-            for i in range(0, GROUP, 2):
+            for i in range(0, GROUP, WIDE):
                 block = jnp.concatenate(
-                    [keys_t[:, at(key_list[base + i])], keys_t[:, at(key_list[base + i + 1])]], axis=1
+                    [query_key[at(plan[0, r, base + i + k]), HDIM:] for k in range(WIDE)], axis=0
                 )
-                found = jnp.dot(queries[j], block, preferred_element_type=jnp.float32)
-                scores[lax.rem(stage, 2), g, j, :, i * TILE : (i + 2) * TILE] = found
-                peak = jnp.maximum(peak, jnp.maximum(found[:, :TILE], found[:, TILE:]))
+                found = lax.dot_general(
+                    queries[j], block, (((1,), (1,)), ((), ())), preferred_element_type=jnp.float32
+                )
+                scores[lax.rem(stage, 2), g, j, :, i * TILE : (i + WIDE) * TILE] = found
+                for k in range(WIDE):
+                    peak = jnp.maximum(peak, found[:, k * TILE : (k + 1) * TILE])
             fresh.append(peak)
         return tuple(fresh)
 
     def value_step(stage, g, row_peaks, totals):
         fresh = []
         for j in range(TOGETHER):
-            base = (stage * TOGETHER + j) * pad + g * GROUP
+            r, base = stage * TOGETHER + j, g * GROUP
             weight = jnp.exp2(
                 scores[lax.rem(stage, 2), g, j] * factor - row_peaks[j]
             ).astype(jnp.bfloat16)
-            block = jnp.concatenate([values[at(value_list[base + i]), :] for i in range(GROUP)], axis=0)
+            block = jnp.concatenate([values[at(plan[1, r, base + i]), :] for i in range(GROUP)], axis=0)
             fresh.append(totals[j] + jnp.dot(weight, block, preferred_element_type=jnp.float32))
         return tuple(fresh)
 
+    def tile_of(stage, j):
+        return plan[2, stage * TOGETHER + j, 0]
+
     def load_queries(stage):
-        return [qkv_ref[at(order[stage * TOGETHER + j]), :HDIM] for j in range(TOGETHER)]
+        return [query_key[at(tile_of(stage, j)), :HDIM] for j in range(TOGETHER)]
 
     def steps_of(stage):
-        return (counts[stage * TOGETHER] + GROUP - 1) // GROUP
+        return (plan[2, stage * TOGETHER, 1] + GROUP - 1) // GROUP
 
     def to_rows(peaks):
-        return tuple(
-            jnp.broadcast_to(jnp.max(peak, axis=1, keepdims=True) * factor, (TILE, 1)) for peak in peaks
-        )
+        return tuple(jnp.max(peak, axis=1, keepdims=True) * factor for peak in peaks)
 
     def finish(stage, totals):
         for j in range(TOGETHER):
-            out_ref[at(order[stage * TOGETHER + j]), :] = (
+            out_ref[at(tile_of(stage, j)), :] = (
                 totals[j][:, :HDIM] / totals[j][:, HDIM:]
             ).astype(jnp.bfloat16)
 
     low = tuple(jnp.full((TILE, TILE), -jnp.inf, jnp.float32) for _ in range(TOGETHER))
     zero = tuple(jnp.zeros((TILE, 2 * HDIM), jnp.float32) for _ in range(TOGETHER))
 
-    @pl.when(counts[tiles] == 1)
+    @pl.when(is_active())
     def _():
-        def prepare(t, carry):
-            keys_t[:, at(t)] = qkv_ref[at(t), HDIM : 2 * HDIM].T
-            values[at(t), :HDIM] = qkv_ref[at(t), 2 * HDIM :]
-            values[at(t), HDIM:] = jnp.ones((TILE, HDIM), jnp.bfloat16)
-            return carry
-
-        lax.fori_loop(0, tiles, prepare, 0, unroll=2)
-        values[pl.ds(tiles * TILE, TILE), :] = jnp.zeros((TILE, 2 * HDIM), jnp.bfloat16)
+        loads = [
+            pltpu.make_async_copy(qkv_ref.at[:, : 2 * HDIM], query_key, load_sem.at[0]),
+            pltpu.make_async_copy(
+                qkv_ref.at[:, 2 * HDIM :], values.at[pl.ds(0, tokens), pl.ds(0, HDIM)], load_sem.at[1]
+            ),
+        ]
+        for load in loads:
+            load.start()
+        make_plan()
+        values[pl.ds(0, tokens), HDIM:] = jnp.ones((tokens, HDIM), jnp.bfloat16)
+        values[pl.ds(tokens, TILE), :] = jnp.zeros((TILE, 2 * HDIM), jnp.bfloat16)
+        for load in loads:
+            load.wait()
 
         queries = load_queries(0)
         peaks = lax.fori_loop(0, steps_of(0), lambda g, p: score_step(queries, 0, g, p), low)
@@ -110,56 +155,33 @@
         finish(stages - 1, totals)
 
 
-def attend(order, key_list, value_list, counts, qkv):
+def attend(is_active, tile_slot, tile_mask, qkv):
     rows = qkv.shape[0]
+    tiles = rows // TILE
     return pl.pallas_call(
-        attend_kernel,
+        functools.partial(attend_kernel, is_active),
         out_shape=jax.ShapeDtypeStruct((rows, HDIM), jnp.bfloat16),
-        grid_spec=pltpu.PrefetchScalarGridSpec(
-            num_scalar_prefetch=4,
-            grid=(1,),
-            in_specs=[pl.BlockSpec((rows, 3 * HDIM), lambda i, *_: (0, 0))],
-            out_specs=pl.BlockSpec((rows, HDIM), lambda i, *_: (0, 0)),
-            scratch_shapes=[
-                pltpu.VMEM((HDIM, rows), jnp.bfloat16),
-                pltpu.VMEM((rows + TILE, 2 * HDIM), jnp.bfloat16),
-                pltpu.VMEM(
-                    (2, rows // (TILE * GROUP), TOGETHER, TILE, GROUP * TILE), jnp.float32
-                ),
-            ],
-        ),
-        compiler_params=pltpu.CompilerParams(vmem_limit_bytes=52 * 1024 * 1024),
+        in_specs=[
+            pl.BlockSpec(memory_space=pltpu.VMEM),
+            pl.BlockSpec(memory_space=pltpu.VMEM),
+            pl.BlockSpec(memory_space=pl.ANY),
+        ],
+        out_specs=pl.BlockSpec(memory_space=pltpu.VMEM),
+        scratch_shapes=[
+            pltpu.VMEM((rows, 2 * HDIM), jnp.bfloat16),
+            pltpu.VMEM((rows + TILE, 2 * HDIM), jnp.bfloat16),
+            pltpu.VMEM((2, -(-tiles // GROUP), TOGETHER, TILE, GROUP * TILE), jnp.float32),
+            pltpu.VMEM((3, tiles, 128), jnp.int32),
+            pltpu.SMEM((3, tiles, 128), jnp.int32),
+            pltpu.SemaphoreType.DMA((2,)),
+            pltpu.SemaphoreType.DMA,
+        ],
+        compiler_params=pltpu.CompilerParams(vmem_limit_bytes=60 * 1024 * 1024),
         cost_estimate=pl.CostEstimate(
             flops=4 * rows * rows * HDIM, bytes_accessed=8 * rows * HDIM, transcendentals=rows * rows
         ),
         name="attend",
-    )(order, key_list, value_list, counts, qkv)
-
-
-def live_lists(tile_slot, tile_mask, active):
-    tiles = tile_slot.shape[0]
-    places = jnp.arange(tiles, dtype=jnp.int32)
-    pick = (tile_slot[:, None] == places[None, :]).astype(jnp.float32)
-    mask = (tile_mask == 1).astype(jnp.float32)
-    size = jnp.sum(mask, axis=1)
-    ahead = (size[None, :] > size[:, None]) | (
-        (size[None, :] == size[:, None]) & (places[None, :] < places[:, None])
-    )
-    position = jnp.sum(ahead.astype(jnp.int32), axis=1)
-    arrange = (position[None, :] == places[:, None]).astype(jnp.float32)
-    chosen = jnp.dot(arrange, pick.T)
-    order = jnp.sum(chosen * places[None, :].astype(jnp.float32), axis=1).astype(jnp.int32)
-    live = jnp.dot(jnp.dot(arrange, mask), pick.T)
-    upper = (places[:, None] <= places[None, :]).astype(jnp.float32)
-    rank = jnp.dot(live, upper).astype(jnp.int32) - 1
-    counts = rank[:, -1] + 1
-    hit = (rank[:, :, None] == places[None, None, :]) & (live[:, :, None] > 0.5)
-    listed = jnp.sum(jnp.where(hit, places[None, :, None], 0), axis=1)
-    used = places[None, :] < counts[:, None]
-    key_list = jnp.where(used, listed, listed[:, :1]).reshape(-1)
-    value_list = jnp.where(used, listed, tiles).reshape(-1)
-    counts = jnp.concatenate([counts, active.astype(jnp.int32)[None]])
-    return order, key_list, value_list, counts
+    )(tile_slot.reshape(1, tiles), tile_mask, qkv)
 
 
 def head_slot(head):
@@ -365,7 +387,7 @@
             dma,
         ],
         compiler_params=pltpu.CompilerParams(
-            collective_id=0, has_side_effects=True, vmem_limit_bytes=40 * 1024 * 1024
+            collective_id=0, has_side_effects=True, vmem_limit_bytes=60 * 1024 * 1024
         ),
         cost_estimate=pl.CostEstimate(
             flops=6 * tokens * depth * columns, bytes_accessed=8 * depth * columns, transcendentals=0
@@ -577,7 +599,7 @@
             dma((2, chunks)),
         ],
         compiler_params=pltpu.CompilerParams(
-            collective_id=1, has_side_effects=True, vmem_limit_bytes=40 * 1024 * 1024
+            collective_id=1, has_side_effects=True, vmem_limit_bytes=60 * 1024 * 1024
         ),
         cost_estimate=pl.CostEstimate(
             flops=2 * tokens * depth * columns, bytes_accessed=2 * depth * columns, transcendentals=0
@@ -588,15 +610,14 @@
 
 def body(patch_rows, query_weight, key_weight, value_weight, output_weight, tile_slot, tile_mask):
     groups = lax.axis_size("ctx")
-    shard = lax.axis_index("ctx")
     tokens = patch_rows.shape[0]
     ring = lax.axis_size("head")
-    heads = query_weight.shape[1] // HDIM
-    shift = lax.rem(lax.axis_index("dp"), 2)
-    active = lax.rem(shard + groups - shift, 4) != 3
-    order, key_list, value_list, counts = live_lists(tile_slot, tile_mask, active)
     sent = front(groups, ring, patch_rows, query_weight, key_weight, value_weight)
-    attended = attend(order, key_list, value_list, counts, sent.reshape(groups * tokens, 3 * HDIM))
+
+    def is_active():
+        return whereabouts(groups, ring)[-1]
+
+    attended = attend(is_active, tile_slot, tile_mask, sent.reshape(groups * tokens, 3 * HDIM))
     return back(groups, ring, attended.reshape(groups, tokens, HDIM), output_weight)
 
 

time: 186 us -> 183 us (0.984)
  the two profiles are of different devices: /device:TPU:21 before, /device:TPU:1 now
where the time goes in v4:
time: 183 us; the launch traced here: 182 us
  Pallas kernels  180 us (98%)
  local copies, waits for them, and re-layouts  2.36 us (1%)
    pallas_call x1, Pallas kernels, back(): pl.pallas_call(functools.partial(back_kernel, groups, ring, heads), out_s...  102 us
    pallas_call x1, Pallas kernels, front(): pl.pallas_call(functools.partial(front_kernel, groups, ring, heads), out_...  76 us

profile of v4, /device:TPU:1, one launch (start us, length us, event | category | flops | bytes accessed | tf_op | source)
XLA Modules:
  0.0 182.4 jit_solution(3430680202852590630)
XLA Ops:
  0.0 76.0 %front.1 = bf16[8,768,384]{2,1,0:T(8,128)(2,1)} custom-call(bf16[768,768]{1,0:T(8,128)(2,1)} %patch_ref.1, bf16[3072,768]{1,0:T(8,128)(2,1)} %wq_ref.1, bf16[3072,768]{1,0:T(8,128)(2,1)} %wk_ref.1, bf16[3072,768]{1,0:T(8,128)(2,1)} %wv_ref.1), custom_call_target="tpu_custom_call" | custom-call | flops 10871635968 | bytes 18874368 | tf_op jit(solution)/shard_map/front/pallas_call | solution.py:370
  76.1 2.0 %attend.1 = bf16[6144,128]{1,0:T(8,128)(2,1)} custom-call(s32[1,48]{1,0:T(1,128)} %bitcast.3, s32[48,48]{1,0:T(8,128)} %mask_ref.1, bf16[6144,384]{1,0:T(8,128)(2,1)} %bitcast.4), custom_call_target="tpu_custom_call" | custom-call | flops 19327352832 | bytes 6291456 | tf_op jit(solution)/shard_map/attend/pallas_call | solution.py:161
  78.0 102.0 %back.1 = bf16[768,768]{1,0:T(8,128)(2,1)} custom-call(bf16[8,768,128]{2,1,0:T(8,128)(2,1)} %bitcast.5, bf16[768,3072]{1,0:T(8,128)(2,1)} %wo_ref.1), custom_call_target="tpu_custom_call" | custom-call | flops 3623878656 | bytes 4718592 | tf_op jit(solution)/shard_map/back/pallas_call | solution.py:578
  180.0 2.4 %copy.9 = bf16[768,768]{1,0:T(8,128)(2,1)} copy(bf16[768,768]{1,0:T(8,128)(2,1)} %back.1) | data formatting | bytes 2359296

commit v5 on v4

--- a/solution.py
+++ b/solution.py
@@ -13,9 +13,12 @@
 GROUP = 8
 TOGETHER = 3
 WIDE = 2
-FRONT_ROWS = 128
+FRONT_ROWS = 64
 FRONT_AHEAD = 2
+FRONT_LAG = 1
+FRONT_ORDER = (1, 2, 3, 4, 5, 6, 7)
 BACK_ROWS = 128
+BACK_LAG = 2
 MESH = pl.DeviceIdType.MESH
 LOG2E = 1.4426950408889634
 
@@ -184,11 +187,7 @@
     )(tile_slot.reshape(1, tiles), tile_mask, qkv)
 
 
-def head_slot(head):
-    return head + head // 3
-
-
-def sync_peers(here, peers):
+def sync_peers(peers):
     barrier = pltpu.get_barrier_semaphore()
     for peer in peers:
         pl.semaphore_signal(barrier, inc=1, device_id=peer, device_id_type=MESH)
@@ -222,7 +221,7 @@
     ]
     for load in loads:
         load.start()
-    sync_peers(ctx, peers)
+    sync_peers(peers)
 
     def span(c):
         return pl.ds(pl.multiple_of(c * chunk, chunk), chunk)
@@ -256,20 +255,24 @@
             device_id_type=MESH,
         )
 
-    def give_copy(c, h):
-        target = lax.rem(head_slot(h) + shift, groups)
-        return target, pltpu.make_async_remote_copy(
-            src_ref=stage.at[h, span(c), :],
+    def give_copy(c, i):
+        target = lax.rem(ctx + i, groups)
+        unit = lax.rem(target + groups - shift, groups)
+        owner = jnp.minimum(unit - unit // 4, heads - 1)
+        return lax.rem(unit, 4) != 3, pltpu.make_async_remote_copy(
+            src_ref=stage.at[owner, span(c), :],
             dst_ref=out_ref.at[ctx, span(c), :],
-            send_sem=give_sem.at[h, c],
+            send_sem=give_sem.at[i - 1, c],
             recv_sem=take_sem,
             device_id=(target, head, part),
             device_id_type=MESH,
         )
 
-    def keep_copy(c, h):
+    def keep_copy(c):
+        unit = lax.rem(ctx + groups - shift, groups)
+        owner = jnp.minimum(unit - unit // 4, heads - 1)
         return pltpu.make_async_copy(
-            stage.at[h, span(c), :], out_ref.at[ctx, span(c), :], self_sem.at[c]
+            stage.at[owner, span(c), :], out_ref.at[ctx, span(c), :], self_sem.at[c]
         )
 
     def project_chunk(c):
@@ -290,17 +293,16 @@
                     stage[2 * pair + j, span(c), i * HDIM : (i + 1) * HDIM] = total[
                         :, j * HDIM : (j + 1) * HDIM
                     ]
-            for j in range(2):
-                h = 2 * pair + j
-                target, copy = give_copy(c, h)
-
-                @pl.when(target != ctx)
-                def _():
-                    copy.start()
-
-                @pl.when(target == ctx)
-                def _():
-                    keep_copy(c, h).start()
+        for i in FRONT_ORDER:
+            owned, copy = give_copy(c, i)
+
+            @pl.when(owned)
+            def _():
+                copy.start()
+
+        @pl.when(active)
+        def _():
+            keep_copy(c).start()
 
     ahead = min(FRONT_AHEAD, chunks)
     for c in range(ahead):
@@ -327,29 +329,29 @@
         def _():
             send_own(c + ahead)
 
-        @pl.when(c > 0)
-        def _():
-            arrival(across, c - 1, far_sem).wait()
-            project_chunk(c - 1)
+        @pl.when(c >= FRONT_LAG)
+        def _():
+            arrival(across, c - FRONT_LAG, far_sem).wait()
+            project_chunk(c - FRONT_LAG)
 
         return carry
 
-    lax.fori_loop(0, chunks + 1, step, 0)
+    lax.fori_loop(0, chunks + FRONT_LAG, step, 0)
 
     def settle(c, carry):
         own_copy(c, 0, right, left_sem).wait_send()
         own_copy(c, 1, left, right_sem).wait_send()
         pass_copy(c, left, right).wait_send()
-        for h in range(heads):
-            target, copy = give_copy(c, h)
-
-            @pl.when(target != ctx)
+        for i in range(1, groups):
+            owned, copy = give_copy(c, i)
+
+            @pl.when(owned)
             def _():
                 copy.wait_send()
 
-            @pl.when(target == ctx)
-            def _():
-                keep_copy(c, h).wait()
+        @pl.when(active)
+        def _():
+            keep_copy(c).wait()
 
         return carry
 
@@ -382,7 +384,7 @@
             dma((chunks,)),
             dma((chunks,)),
             dma((chunks,)),
-            dma((heads, chunks)),
+            dma((groups - 1, chunks)),
             dma((chunks,)),
             dma,
         ],
@@ -419,7 +421,7 @@
     ]
     for load in loads:
         load.start()
-    sync_peers(ctx, peers)
+    sync_peers(peers)
 
     def span(c):
         return pl.ds(pl.multiple_of(c * chunk, chunk), chunk)
@@ -537,21 +539,21 @@
         ).astype(jnp.bfloat16)
 
     def step(c, carry):
-        @pl.when((c > 0) & (c <= chunks))
-        def _():
-            merge(c - 1)
+        @pl.when((c >= BACK_LAG) & (c < chunks + BACK_LAG))
+        def _():
+            merge(c - BACK_LAG)
 
         @pl.when(c < chunks)
         def _():
             mix(c)
 
-        @pl.when(c > 1)
-        def _():
-            close(c - 2)
+        @pl.when(c >= 2 * BACK_LAG)
+        def _():
+            close(c - 2 * BACK_LAG)
 
         return carry
 
-    lax.fori_loop(0, chunks + 2, step, 0)
+    lax.fori_loop(0, chunks + 2 * BACK_LAG, step, 0)
 
     def settle(c, carry):
         far_copy(c, right).wait_send()

time: 183 us -> 162 us (0.89)
  Pallas kernels: 180 us -> 159 us
    pallas_call x1, Pallas kernels: 102 us -> 86.2 us  [back(): pl.pallas_call(functools.partial(back_kernel, groups, ring, heads), out_s...]
    pallas_call x1, Pallas kernels: 76 us -> 70.7 us  [front(): pl.pallas_call(functools.partial(front_kernel, groups, ring, heads), out_...]
where the time goes in v5:
time: 162 us; the launch traced here: 161 us
  Pallas kernels  159 us (98%)
  local copies, waits for them, and re-layouts  2.36 us (1%)
    pallas_call x1, Pallas kernels, back(): pl.pallas_call(functools.partial(back_kernel, groups, ring, heads), out_s...  86.2 us
    pallas_call x1, Pallas kernels, front(): pl.pallas_call(functools.partial(front_kernel, groups, ring, heads), out_...  70.7 us

profile of v5, /device:TPU:1, one launch (start us, length us, event | category | flops | bytes accessed | tf_op | source)
XLA Modules:
  0.0 161.3 jit_solution(12446403797096030358)
XLA Ops:
  0.0 70.7 %front.1 = bf16[8,768,384]{2,1,0:T(8,128)(2,1)} custom-call(bf16[768,768]{1,0:T(8,128)(2,1)} %patch_ref.1, bf16[3072,768]{1,0:T(8,128)(2,1)} %wq_ref.1, bf16[3072,768]{1,0:T(8,128)(2,1)} %wk_ref.1, bf16[3072,768]{1,0:T(8,128)(2,1)} %wv_ref.1), custom_call_target="tpu_custom_call" | custom-call | flops 10871635968 | bytes 18874368 | tf_op jit(solution)/shard_map/front/pallas_call | solution.py:372
  70.7 2.0 %attend.1 = bf16[6144,128]{1,0:T(8,128)(2,1)} custom-call(s32[1,48]{1,0:T(1,128)} %bitcast.3, s32[48,48]{1,0:T(8,128)} %mask_ref.1, bf16[6144,384]{1,0:T(8,128)(2,1)} %bitcast.4), custom_call_target="tpu_custom_call" | custom-call | flops 19327352832 | bytes 6291456 | tf_op jit(solution)/shard_map/attend/pallas_call | solution.py:164
  72.7 86.2 %back.1 = bf16[768,768]{1,0:T(8,128)(2,1)} custom-call(bf16[8,768,128]{2,1,0:T(8,128)(2,1)} %bitcast.5, bf16[768,3072]{1,0:T(8,128)(2,1)} %wo_ref.1), custom_call_target="tpu_custom_call" | custom-call | flops 3623878656 | bytes 4718592 | tf_op jit(solution)/shard_map/back/pallas_call | solution.py:580
  158.9 2.4 %copy.9 = bf16[768,768]{1,0:T(8,128)(2,1)} copy(bf16[768,768]{1,0:T(8,128)(2,1)} %back.1) | data formatting | bytes 2359296

commit v6 on v5

--- a/solution.py
+++ b/solution.py
@@ -10,9 +10,9 @@
 
 HDIM = 128
 TILE = 128
-GROUP = 8
+GROUP = 12
 TOGETHER = 3
-WIDE = 2
+WIDE = 6
 FRONT_ROWS = 64
 FRONT_AHEAD = 2
 FRONT_LAG = 1
@@ -69,12 +69,12 @@
         move.start()
         move.wait()
 
-    def score_step(queries, stage, g, peaks):
+    def score_step(queries, stage, g, peaks, size=GROUP):
         fresh = []
         for j in range(TOGETHER):
             r, base = stage * TOGETHER + j, g * GROUP
             peak = peaks[j]
-            for i in range(0, GROUP, WIDE):
+            for i in range(0, size, WIDE):
                 block = jnp.concatenate(
                     [query_key[at(plan[0, r, base + i + k]), HDIM:] for k in range(WIDE)], axis=0
                 )
@@ -87,14 +87,14 @@
             fresh.append(peak)
         return tuple(fresh)
 
-    def value_step(stage, g, row_peaks, totals):
+    def value_step(stage, g, row_peaks, totals, size=GROUP):
         fresh = []
         for j in range(TOGETHER):
             r, base = stage * TOGETHER + j, g * GROUP
             weight = jnp.exp2(
-                scores[lax.rem(stage, 2), g, j] * factor - row_peaks[j]
+                scores[lax.rem(stage, 2), g, j, :, : size * TILE] * factor - row_peaks[j]
             ).astype(jnp.bfloat16)
-            block = jnp.concatenate([values[at(plan[1, r, base + i]), :] for i in range(GROUP)], axis=0)
+            block = jnp.concatenate([values[at(plan[1, r, base + i]), :] for i in range(size)], axis=0)
             fresh.append(totals[j] + jnp.dot(weight, block, preferred_element_type=jnp.float32))
         return tuple(fresh)
 
@@ -104,8 +104,12 @@
     def load_queries(stage):
         return [query_key[at(tile_of(stage, j)), :HDIM] for j in range(TOGETHER)]
 
-    def steps_of(stage):
-        return (plan[2, stage * TOGETHER, 1] + GROUP - 1) // GROUP
+    def over_steps(stage, step, carry):
+        half = GROUP // 2
+        halves = (plan[2, stage * TOGETHER, 1] + half - 1) // half
+        whole = halves // 2
+        carry = lax.fori_loop(0, whole, lambda g, c: step(g, c, GROUP), carry)
+        return lax.fori_loop(whole, halves - whole, lambda g, c: step(g, c, half), carry)
 
     def to_rows(peaks):
         return tuple(jnp.max(peak, axis=1, keepdims=True) * factor for peak in peaks)
@@ -136,24 +140,24 @@
             load.wait()
 
         queries = load_queries(0)
-        peaks = lax.fori_loop(0, steps_of(0), lambda g, p: score_step(queries, 0, g, p), low)
+        peaks = over_steps(0, lambda g, p, size: score_step(queries, 0, g, p, size), low)
 
         def stage_body(stage, row_peaks):
             queries = load_queries(stage)
 
-            def both(g, carry):
+            def both(g, carry, size):
                 peaks, totals = carry
-                totals = value_step(stage - 1, g, row_peaks, totals)
-                peaks = score_step(queries, stage, g, peaks)
+                totals = value_step(stage - 1, g, row_peaks, totals, size)
+                peaks = score_step(queries, stage, g, peaks, size)
                 return peaks, totals
 
-            peaks, totals = lax.fori_loop(0, steps_of(stage - 1), both, (low, zero))
+            peaks, totals = over_steps(stage - 1, both, (low, zero))
             finish(stage - 1, totals)
             return to_rows(peaks)
 
         row_peaks = lax.fori_loop(1, stages, stage_body, to_rows(peaks))
-        totals = lax.fori_loop(
-            0, steps_of(stages - 1), lambda g, t: value_step(stages - 1, g, row_peaks, t), zero
+        totals = over_steps(
+            stages - 1, lambda g, t, size: value_step(stages - 1, g, row_peaks, t, size), zero
         )
         finish(stages - 1, totals)
 
@@ -179,7 +183,7 @@
             pltpu.SemaphoreType.DMA((2,)),
             pltpu.SemaphoreType.DMA,
         ],
-        compiler_params=pltpu.CompilerParams(vmem_limit_bytes=60 * 1024 * 1024),
+        compiler_params=pltpu.CompilerParams(vmem_limit_bytes=56 * 1024 * 1024),
         cost_estimate=pl.CostEstimate(
             flops=4 * rows * rows * HDIM, bytes_accessed=8 * rows * HDIM, transcendentals=rows * rows
         ),
@@ -245,14 +249,23 @@
         own_copy(c, 0, right, left_sem).start()
         own_copy(c, 1, left, right_sem).start()
 
-    def pass_copy(c, slot, to):
+    def half(c, i):
+        return pl.ds(pl.multiple_of(c * chunk + i * (chunk // 2), chunk // 2), chunk // 2)
+
+    def pass_copy(c, i):
+        slot, to = ((left, right), (right, left))[i]
         return pltpu.make_async_remote_copy(
-            src_ref=rows_all.at[slot, span(c), :],
-            dst_ref=rows_all.at[slot, span(c), :],
-            send_sem=pass_sem.at[c],
-            recv_sem=far_sem.at[c],
+            src_ref=rows_all.at[slot, half(c, i), :],
+            dst_ref=rows_all.at[slot, half(c, i), :],
+            send_sem=pass_sem.at[i, c],
+            recv_sem=far_sem.at[i, c],
             device_id=(ctx, to, part),
             device_id_type=MESH,
+        )
+
+    def far_arrival(c, i):
+        return pltpu.make_async_copy(
+            rows_all.at[across, half(c, i), :], rows_all.at[across, half(c, i), :], far_sem.at[i, c]
         )
 
     def give_copy(c, i):
@@ -308,30 +321,29 @@
     for c in range(ahead):
         send_own(c)
     rows_all[head] = patch_ref[...]
-    for load in loads:
-        load.wait()
 
     def step(c, carry):
         @pl.when(c < chunks)
         def _():
             arrival(left, c, left_sem).wait()
+            pass_copy(c, 0).start()
             arrival(right, c, right_sem).wait()
-
-            @pl.when(lax.rem(c, 2) == 0)
+            pass_copy(c, 1).start()
+
+        @pl.when(c + ahead < chunks)
+        def _():
+            send_own(c + ahead)
+
+        @pl.when(c >= FRONT_LAG)
+        def _():
+            for i in range(2):
+                far_arrival(c - FRONT_LAG, i).wait()
+
+            @pl.when(c == FRONT_LAG)
             def _():
-                pass_copy(c, left, right).start()
-
-            @pl.when(lax.rem(c, 2) == 1)
-            def _():
-                pass_copy(c, right, left).start()
-
-        @pl.when(c + ahead < chunks)
-        def _():
-            send_own(c + ahead)
-
-        @pl.when(c >= FRONT_LAG)
-        def _():
-            arrival(across, c - FRONT_LAG, far_sem).wait()
+                for load in loads:
+                    load.wait()
+
             project_chunk(c - FRONT_LAG)
 
         return carry
@@ -341,7 +353,8 @@
     def settle(c, carry):
         own_copy(c, 0, right, left_sem).wait_send()
         own_copy(c, 1, left, right_sem).wait_send()
-        pass_copy(c, left, right).wait_send()
+        pass_copy(c, 0).wait_send()
+        pass_copy(c, 1).wait_send()
         for i in range(1, groups):
             owned, copy = give_copy(c, i)
 
@@ -382,8 +395,8 @@
             dma((2, chunks)),
             dma((chunks,)),
             dma((chunks,)),
-            dma((chunks,)),
-            dma((chunks,)),
+            dma((2, chunks)),
+            dma((2, chunks)),
             dma((groups - 1, chunks)),
             dma((chunks,)),
             dma,
@@ -452,23 +465,26 @@
 
         lax.fori_loop(0, chunks, give, 0)
 
-    def far_copy(c, to):
+    def half(c, i):
+        return pl.ds(pl.multiple_of(c * chunk + i * (chunk // 2), chunk // 2), chunk // 2)
+
+    def far_copy(c, i):
         return pltpu.make_async_remote_copy(
-            src_ref=far_out.at[span(c), :],
-            dst_ref=far_in.at[span(c), :],
-            send_sem=far_send.at[c],
-            recv_sem=far_recv.at[c],
-            device_id=(ctx, to, part),
+            src_ref=far_out.at[half(c, i), :],
+            dst_ref=far_in.at[half(c, i), :],
+            send_sem=far_send.at[i, c],
+            recv_sem=far_recv.at[i, c],
+            device_id=(ctx, (right, left)[i], part),
             device_id_type=MESH,
         )
 
-    def side_copy(c, way, to):
+    def side_copy(c, way, i):
         return pltpu.make_async_remote_copy(
-            src_ref=side_out.at[way, span(c), :],
-            dst_ref=side_in.at[way, span(c), :],
-            send_sem=side_send.at[way, c],
-            recv_sem=side_recv.at[way, c],
-            device_id=(ctx, to, part),
+            src_ref=side_out.at[way, half(c, i), :],
+            dst_ref=side_in.at[way, half(c, i), :],
+            send_sem=side_send.at[2 * way + i, c],
+            recv_sem=side_recv.at[2 * way + i, c],
+            device_id=(ctx, (right, left)[way], part),
             device_id_type=MESH,
         )
 
@@ -496,42 +512,30 @@
             return jnp.dot(rows, weights[i], preferred_element_type=jnp.float32)
 
         far_out[span(c), :] = part_sum(0).astype(jnp.bfloat16)
-        even = lax.rem(c, 2) == 0
-
-        @pl.when(even)
-        def _():
-            far_copy(c, right).start()
-            side_out[1, span(c), :] = part_sum(2).astype(jnp.bfloat16)
-            side_copy(c, 1, left).start()
-            pending[span(c), :] = part_sum(1)
-
-        @pl.when(jnp.logical_not(even))
-        def _():
-            far_copy(c, left).start()
-            side_out[0, span(c), :] = part_sum(1).astype(jnp.bfloat16)
-            side_copy(c, 0, right).start()
-            pending[span(c), :] = part_sum(2)
-
+        far_copy(c, 0).start()
+        far_copy(c, 1).start()
+        middle = chunk // 2
+        to_right, to_left = part_sum(1), part_sum(2)
+        side_out[0, half(c, 1), :] = to_right[middle:].astype(jnp.bfloat16)
+        side_copy(c, 0, 1).start()
+        side_out[1, half(c, 0), :] = to_left[:middle].astype(jnp.bfloat16)
+        side_copy(c, 1, 0).start()
+        pending[half(c, 0), :] = to_right[:middle]
+        pending[half(c, 1), :] = to_left[middle:]
         own[span(c), :] = part_sum(3)
 
     def merge(c):
-        far_copy(c, right).wait_recv()
-        merged = (pending[span(c), :] + far_in[span(c), :].astype(jnp.float32)).astype(jnp.bfloat16)
-        even = lax.rem(c, 2) == 0
-
-        @pl.when(even)
-        def _():
-            side_out[0, span(c), :] = merged
-            side_copy(c, 0, right).start()
-
-        @pl.when(jnp.logical_not(even))
-        def _():
-            side_out[1, span(c), :] = merged
-            side_copy(c, 1, left).start()
+        for i in range(2):
+            far_copy(c, i).wait_recv()
+            side_out[i, half(c, i), :] = (
+                pending[half(c, i), :] + far_in[half(c, i), :].astype(jnp.float32)
+            ).astype(jnp.bfloat16)
+            side_copy(c, i, i).start()
 
     def close(c):
-        side_copy(c, 0, right).wait_recv()
-        side_copy(c, 1, left).wait_recv()
+        for way in range(2):
+            for i in range(2):
+                side_copy(c, way, i).wait_recv()
         out_ref[span(c), :] = (
             own[span(c), :]
             + side_in[0, span(c), :].astype(jnp.float32)
@@ -556,9 +560,10 @@
     lax.fori_loop(0, chunks + 2 * BACK_LAG, step, 0)
 
     def settle(c, carry):
-        far_copy(c, right).wait_send()
-        side_copy(c, 0, right).wait_send()
-        side_copy(c, 1, left).wait_send()
+        for i in range(2):
+            far_copy(c, i).wait_send()
+            side_copy(c, 0, i).wait_send()
+            side_copy(c, 1, i).wait_send()
 
         @pl.when(active)
         def _():
@@ -595,10 +600,10 @@
             dma((groups - 1, chunks)),
             dma((chunks,)),
             dma((chunks,)),
-            dma((chunks,)),
-            dma((chunks,)),
             dma((2, chunks)),
             dma((2, chunks)),
+            dma((4, chunks)),
+            dma((4, chunks)),
         ],
         compiler_params=pltpu.CompilerParams(
             collective_id=1, has_side_effects=True, vmem_limit_bytes=60 * 1024 * 1024

time: 162 us -> 159 us (0.981)
  Pallas kernels: 159 us -> 156 us
    pallas_call x1, Pallas kernels: 86.2 us -> 84.1 us  [back(): pl.pallas_call(functools.partial(back_kernel, groups, ring, heads), out_s...]
where the time goes in v6:
time: 159 us; the launch traced here: 158 us
  Pallas kernels  156 us (98%)
  local copies, waits for them, and re-layouts  2.36 us (1%)
    pallas_call x1, Pallas kernels, back(): pl.pallas_call(functools.partial(back_kernel, groups, ring, heads), out_s...  84.1 us
    pallas_call x1, Pallas kernels, front(): pl.pallas_call(functools.partial(front_kernel, groups, ring, heads), out_...  70.1 us

profile of v6, /device:TPU:1, one launch (start us, length us, event | category | flops | bytes accessed | tf_op | source)
XLA Modules:
  0.0 158.5 jit_solution(15866113437738589102)
XLA Ops:
  0.0 70.1 %front.1 = bf16[8,768,384]{2,1,0:T(8,128)(2,1)} custom-call(bf16[768,768]{1,0:T(8,128)(2,1)} %patch_ref.1, bf16[3072,768]{1,0:T(8,128)(2,1)} %wq_ref.1, bf16[3072,768]{1,0:T(8,128)(2,1)} %wk_ref.1, bf16[3072,768]{1,0:T(8,128)(2,1)} %wv_ref.1), custom_call_target="tpu_custom_call" | custom-call | flops 10871635968 | bytes 18874368 | tf_op jit(solution)/shard_map/front/pallas_call | solution.py:385
  70.1 2.0 %attend.1 = bf16[6144,128]{1,0:T(8,128)(2,1)} custom-call(s32[1,48]{1,0:T(1,128)} %bitcast.3, s32[48,48]{1,0:T(8,128)} %mask_ref.1, bf16[6144,384]{1,0:T(8,128)(2,1)} %bitcast.4), custom_call_target="tpu_custom_call" | custom-call | flops 19327352832 | bytes 6291456 | tf_op jit(solution)/shard_map/attend/pallas_call | solution.py:168
  72.0 84.1 %back.1 = bf16[768,768]{1,0:T(8,128)(2,1)} custom-call(bf16[8,768,128]{2,1,0:T(8,128)(2,1)} %bitcast.5, bf16[768,3072]{1,0:T(8,128)(2,1)} %wo_ref.1), custom_call_target="tpu_custom_call" | custom-call | flops 3623878656 | bytes 4718592 | tf_op jit(solution)/shard_map/back/pallas_call | solution.py:585
  156.1 2.4 %copy.9 = bf16[768,768]{1,0:T(8,128)(2,1)} copy(bf16[768,768]{1,0:T(8,128)(2,1)} %back.1) | data formatting | bytes 2359296
